TPU v7x, 32 devices: a whole 2x2x4 slice. The times are simulated.
32 devices in a mesh: dp: 8 (over y, x, core), expert: 4 (over z).
Axes of the slice: x: 2, y: 2, z: 4, core: 2. Of those that a mesh axis runs over, the one named last changes fastest.
Arguments:
- hidden_input: bfloat16 [40960, 768], P(('dp', 'expert')), may hold values from -6 to 6
- gate_carryover: float32 [40960, 8], P(('dp', 'expert')), may hold values from -2.5 to 2.5
- sequence_length: int32 [32, 5], P(('dp', 'expert')), may hold values from 1 to 1024, 1280 in all within a row
- token_stream_place: int32 [32, 1280], P(('dp', 'expert')), may hold values from 0 to 1279, each once within a row
- expert_choice_index: int32 [40960, 2], P(('dp', 'expert')), may hold values from 0 to 7, as said below
- sequence_adapter: int32 [32, 5], P(('dp', 'expert')), may hold values from 0 to 7
- attention_gain: bfloat16 [768], replicated, may hold values from 0.25 to 1.75
- query_key_weight: bfloat16 [768, 2304], P(('dp', 'expert')), may hold values from -0.21875 to 0.21875
- output_weight: bfloat16 [768, 768], P(('dp', 'expert')), may hold values from -0.625 to 0.625
- adapter_in_query: bfloat16 [768, 128], P(('dp', 'expert')), may hold values from -0.21875 to 0.21875
- adapter_out_query: bfloat16 [128, 2304], P(('dp', 'expert')), may hold values from -0.5 to 0.5
- adapter_in_output: bfloat16 [768, 128], P(('dp', 'expert')), may hold values from -0.21875 to 0.21875
- adapter_out_output: bfloat16 [128, 768], P(('dp', 'expert')), may hold values from -1.5 to 1.5
- feedfwd_gain: bfloat16 [768], replicated, may hold values from 0.25 to 1.75
- router_weight: bfloat16 [768, 8], replicated, may hold values from -0.15625 to 0.15625
- constant_gate: bfloat16 [768, 4], replicated, may hold values from -0.21875 to 0.21875
- constant_value: bfloat16 [2, 768], replicated, may hold values from -6 to 6
- gate_upward_weight: bfloat16 [4, 768, 4096], P('expert', 'dp'), may hold values from -0.21875 to 0.21875
- down_weight: bfloat16 [4, 2048, 768], P('expert', 'dp'), may hold values from -1.5 to 1.5
- adapter_in_gate: bfloat16 [4, 768, 128], P('expert', 'dp'), may hold values from -0.21875 to 0.21875
- adapter_out_gate: bfloat16 [4, 128, 4096], P('expert', 'dp'), may hold values from -0.5 to 0.5
- adapter_in_down: bfloat16 [4, 2048, 128], P('expert', 'dp'), may hold values from -0.125 to 0.125
- adapter_out_down: bfloat16 [4, 128, 768], P('expert', 'dp'), may hold values from -6 to 6
- output_gradient: bfloat16 [40960, 768], P(('dp', 'expert')), may hold values from -6 to 6
Outputs:
- out_hidden: bfloat16 [40960, 768], P(('dp', 'expert'))
- grad_hidden: float32 [40960, 768], P(('dp', 'expert'))
- grad_gate_res: float32 [40960, 8], P(('dp', 'expert'))
- grad_a_qkv: float32 [768, 128], P(('dp', 'expert'))
- grad_b_qkv: float32 [128, 2304], P(('dp', 'expert'))
- grad_a_out: float32 [768, 128], P(('dp', 'expert'))
- grad_b_out: float32 [128, 768], P(('dp', 'expert'))
- grad_a_gu: float32 [4, 768, 128], P('expert', 'dp')
- grad_b_gu: float32 [4, 128, 4096], P('expert', 'dp')
- grad_a_down: float32 [4, 2048, 128], P('expert', 'dp')
- grad_b_down: float32 [4, 128, 768], P('expert', 'dp')
Inputs may be any that keep to these rules, and one draw needn't show every extreme that they name: `expert_choice_index`: each row names two different experts. Ids under 4 are feed-forward experts, 4 is the zero expert, 5 the copy expert, 6 and 7 the constant experts. Among the rows of one device no id under 4 appears more than 408 times; on every device of one index of dp some such id appears exactly 408 times.
All inputs are finite; a program needn't handle non-finite values.
Results may differ from a plain program's by a relative error of at most 0.019.
Values may be sent and summed in bfloat16 or wider, within the bound.
A program may use at most 384 MiB of HBM per device.

v0:
```python
import functools
import math

import jax
import jax.numpy as jnp
from jax import lax
from jax.experimental import pallas as pl
from jax.experimental.pallas import tpu as pltpu
from jax.sharding import PartitionSpec as P

MODEL_WIDTH = 768
HEAD_COUNT = 12
HEAD_DIM = 64
FEEDFWD_WIDTH = 2048
ADAPTER_RANK = 16
ROW_BLOCK = 256
HIDDEN_BLOCK = 1024
LANES = 128
CONST_LANE = 64
CHOICE_LANE = 48
CHOICE_ROWS = 16
EPSILON = 1e-06
VMEM_BYTES = 60 * 2**20
FRONT_KEPT = 26
MESH_ID = pl.DeviceIdType.MESH

F32 = jnp.float32
BF16 = jnp.bfloat16


def dot(a, b):
    return jnp.dot(a, b, preferred_element_type=F32)


def dot_nt(a, b):
    return lax.dot_general(a, b, (((1,), (1,)), ((), ())), preferred_element_type=F32)


def dot_tn(a, b):
    return lax.dot_general(a, b, (((0,), (0,)), ((), ())), preferred_element_type=F32)


def iota(shape, dim):
    return lax.broadcasted_iota(jnp.int32, shape, dim)


def hot_matrix(condition):
    return jnp.where(condition, 1.0, 0.0).astype(BF16)


def whole(shape):
    zeros = (0,) * len(shape)
    return pl.BlockSpec(shape, lambda *_: zeros)


def row_spec(width, rows=ROW_BLOCK):
    return pl.BlockSpec((rows, width), lambda i: (i, 0))


def col_spec(rows, width=LANES):
    return pl.BlockSpec((rows, width), lambda j: (0, j))


def sds(shape, dtype):
    return jax.ShapeDtypeStruct(shape, dtype)


def call(body, grid, in_specs, out_specs, out_shape, scratch=(), name=None):
    return pl.pallas_call(
        body,
        grid=grid,
        in_specs=in_specs,
        out_specs=out_specs,
        out_shape=out_shape,
        scratch_shapes=list(scratch),
        compiler_params=pltpu.CompilerParams(vmem_limit_bytes=VMEM_BYTES),
        name=name,
    )


def half_swap(values):
    lane = iota(values.shape, 1)
    up = pltpu.roll(values, 32, 1)
    down = pltpu.roll(values, LANES - 32, 1)
    return jnp.where(lane % HEAD_DIM < HEAD_DIM // 2, down, up)


def lane_value(values, lane_id):
    return jnp.sum(jnp.where(iota(values.shape, 1) == lane_id, values, 0.0), axis=1, keepdims=True)


def proj_in_body(
    place_row, hidden, upstream, small, cosine, sine, mask, gain, w_qkv, a_in, b_out,
    hid_s, dy_s, small_s, act_one, low_qkv, query, key, value,
):
    rows = hid_s.shape[0]
    base = pl.program_id(0) * rows
    perm = hot_matrix(place_row[...] == base + iota((rows, place_row.shape[1]), 0))
    hid = dot(perm, hidden[...])
    hid_s[...] = hid.astype(BF16)
    dy_s[...] = dot(perm, upstream[...]).astype(BF16)
    parts = dot(perm, small[...])
    small_s[...] = parts + (pltpu.roll(parts, LANES - 16, 1) + pltpu.roll(parts, LANES - 32, 1))
    act = normed(hid, gain)
    act_one[...] = act
    low, q_val, k_val, value[...] = project(
        act, mask[...], cosine[...], sine[...], w_qkv, a_in, b_out
    )
    low_qkv[...] = low
    query[...], key[...] = q_val, k_val


def normed(values, gain):
    scale = lax.rsqrt(jnp.mean(values * values, axis=-1, keepdims=True) + EPSILON)
    return (values * scale * gain[...].astype(F32)).astype(BF16)


def project(act, mask, cos, sin, w_qkv, a_in, b_out):
    low = (dot(act, a_in[...]) * mask.astype(F32)).astype(BF16)
    turned = []
    for start, factor in ((0, HEAD_DIM**-0.5), (MODEL_WIDTH, 1.0)):
        cols = slice(start, start + MODEL_WIDTH)
        vals = dot(act, w_qkv[:, cols]) + dot(low, b_out[:, cols])
        pieces = []
        for c in range(MODEL_WIDTH // LANES):
            piece = vals[:, c * LANES : (c + 1) * LANES]
            piece = (piece * cos + half_swap(piece) * sin).astype(BF16)
            pieces.append(piece if factor == 1.0 else piece * jnp.asarray(factor, BF16))
        turned.append(jnp.concatenate(pieces, axis=1))
    value = dot(act, w_qkv[:, 2 * MODEL_WIDTH :]) + dot(low, b_out[:, 2 * MODEL_WIDTH :])
    return low, turned[0], turned[1], value.astype(BF16)


def head_mask(shape, head):
    lane = iota(shape, 1)
    return (lane >= head * HEAD_DIM) & (lane < (head + 1) * HEAD_DIM)


def attention_fwd_body(query, key, value, starts, attended, lse):
    attention_fwd_pair(pl.program_id(0), query, key, value, starts, attended, lse)


def visible(lo, hi, starts):
    rows = iota((hi, hi - lo), 0)
    return (rows <= lo + iota((hi, hi - lo), 1)) & (rows >= starts[:, lo:hi])


def attention_fwd_pair(pair, query, key, value, starts, attended, lse):
    size = ROW_BLOCK
    zero = jnp.zeros((), BF16)
    for blk in range(query.shape[0] // size):
        lo, hi = blk * size, (blk + 1) * size
        q_blk = query[lo:hi, :]
        k_all = key[:hi, :]
        v_all = value[:hi, :]
        allowed = visible(lo, hi, starts)
        total = jnp.zeros((size, LANES), F32)
        for head in range(2):
            mine = head_mask((size, LANES), head)
            scores = dot_nt(k_all, jnp.where(mine, q_blk, zero))
            scores = jnp.where(allowed, scores, -1000000000.0)
            top = jnp.max(scores, axis=0, keepdims=True)
            expo = jnp.exp(scores - top)
            norm = jnp.sum(expo, axis=0, keepdims=True)
            prob = (expo * (1.0 / norm)).astype(BF16)
            total = jnp.where(mine, dot_tn(prob, v_all), total)
            lse[pl.ds(2 * pair + head, 1), lo:hi] = top + jnp.log(norm)
        attended[lo:hi, :] = total.astype(BF16)


def attention_bwd_body(
    query, key, value, dout, attended, lse, starts, cosine, sine, d_query, d_key, d_value, kacc, vacc
):
    pair = pl.program_id(0)
    tok = query.shape[0]
    size = ROW_BLOCK
    zero = jnp.zeros((), BF16)
    kacc[...] = jnp.zeros_like(kacc)
    vacc[...] = jnp.zeros_like(vacc)
    for blk in range(tok // size):
        lo, hi = blk * size, (blk + 1) * size
        q_blk = query[lo:hi, :]
        do_blk = dout[lo:hi, :]
        k_all = key[:hi, :]
        v_all = value[:hi, :]
        allowed = visible(lo, hi, starts)
        prod = (do_blk.astype(F32) * attended[lo:hi, :].astype(F32)).T
        probs, dscores, q_heads, do_heads = [], [], [], []
        q_total = jnp.zeros((size, LANES), F32)
        for head in range(2):
            mine = head_mask((size, LANES), head)
            q_heads.append(jnp.where(mine, q_blk, zero))
            do_heads.append(jnp.where(mine, do_blk, zero))
            lse_head = lse[pl.ds(2 * pair + head, 1), lo:hi]
            delta = jnp.sum(
                prod[head * HEAD_DIM : (head + 1) * HEAD_DIM], axis=0, keepdims=True
            )
            scores = dot_nt(k_all, q_heads[head])
            prob = jnp.where(allowed, jnp.exp(scores - lse_head), 0.0)
            dprob = dot_nt(v_all, do_heads[head])
            dscores.append((prob * (dprob - delta)).astype(BF16))
            probs.append(prob.astype(BF16))
            k_head = jnp.where(head_mask((hi, LANES), head), k_all, zero)
            q_total = q_total + dot_tn(dscores[head], k_head)
        kacc[:hi, :] += dot(jnp.concatenate(dscores, axis=1), jnp.concatenate(q_heads, axis=0))
        vacc[:hi, :] += dot(jnp.concatenate(probs, axis=1), jnp.concatenate(do_heads, axis=0))
        q_total = q_total * HEAD_DIM**-0.5
        d_query[lo:hi, :] = (
            q_total * cosine[lo:hi, :] - half_swap(q_total) * sine[lo:hi, :]
        ).astype(BF16)
    for blk in range(tok // size):
        lo, hi = blk * size, (blk + 1) * size
        k_total = kacc[lo:hi, :]
        d_key[lo:hi, :] = (
            k_total * cosine[lo:hi, :] - half_swap(k_total) * sine[lo:hi, :]
        ).astype(BF16)
    d_value[...] = vacc[...].astype(BF16)


def start_kernel(send_to, hear_from, count):
    barrier = pltpu.get_barrier_semaphore()
    for device, remote in hear_from:
        if remote is None:
            pl.semaphore_signal(barrier, inc=1, device_id=device, device_id_type=MESH_ID)
        else:

            @pl.when(remote)
            def _(device=device):
                pl.semaphore_signal(barrier, inc=1, device_id=device, device_id_type=MESH_ID)

    pl.semaphore_wait(barrier, count)


def pair_front_body(
    kinds, a_rows, b_rows,
    lengths, adapters, place_row, hidden, upstream, carry, choices, gain_one, gain_two,
    router_in, const_in, in_qkv, in_out, in_a_qkv, in_a_out, in_b_qkv, in_b_out,
    in_gu, in_b_gu, in_dn, in_b_dn, in_a_gu, in_a_dn, *rest,
):
    count = FRONT_KEPT
    outs, rest = rest[:count], rest[count:]
    (all_wide, all_mid, all_thin, came, last_sent), rest = rest[:5], rest[5:]
    kept, rest = rest[:count], rest[count:]
    (
        hid_s, dy_s, small_s, act_one, low_qkv, mask, starts, cosine, sine, router,
        query, key, value, w_qkv, a_qkv, b_qkv, w_out, a_out, b_out,
        attn_low, lse, low_out, resid, act_two, gate, slot,
    ) = kept
    (
        g_qkv, g_out, own_wide, own_mid, own_thin, sent, slot_rows,
        a_send, a_recv, z_send, e_send, e_recv, out_sems, own_sems, row_send, row_recv,
    ) = rest
    dp, z = lax.axis_index("dp"), lax.axis_index("expert")
    core, x_bit, y_bit = dp % 2, dp // 2 % 2, dp // 4
    across = dp + 1 - 2 * core
    x_dev, y_dev = dp + 2 - 4 * x_bit, dp + 4 - 8 * y_bit
    diag = x_dev + 4 - 8 * y_bit
    far = (z + 2) % 4
    home = z // 2
    columns = (dp, x_dev, y_dev, diag)
    tok = hidden.shape[0]
    blocks = tok // ROW_BLOCK

    def remote(source, target, send, recv, device):
        return pltpu.make_async_remote_copy(
            src_ref=source, dst_ref=target, send_sem=send, recv_sem=recv,
            device_id=device, device_id_type=MESH_ID,
        )

    packs = (g_qkv, g_out)

    def at(kind, back):
        return columns[kind] * 4 + (z + 4 - back) % 4

    def shard(p, kind, back, rows=None):
        view = packs[p].at[at(kind, back)]
        if rows is None:
            return view
        half = packs[p].shape[1] // 2
        return view.at[pl.ds(rows * half, half)]

    def z_up(p, t):
        view = shard(p, 0, t)
        return remote(view, view, z_send.at[p, t], a_recv.at[p, t], (dp, z + 1))

    def z_down(p, t):
        view = shard(p, 0, (4 - t) % 4)
        return remote(view, view, z_send.at[p, 3 + t], a_recv.at[p, 2 - t], (dp, z - 1))

    def z_sends(p, t, act):
        @pl.when((z < 3) & (z >= t))
        def _():
            act(z_up(p, t))

        @pl.when((z > 0) & (z + t <= 3))
        def _():
            act(z_down(p, t))

    def to_x(p, back):
        return remote(
            shard(p, 0, back), shard(p, 0, back), a_send.at[p, 3 + back], a_recv.at[p, 3 + back],
            (x_dev, z),
        )

    def to_y(p, back):
        return remote(
            shard(p, 0, back), shard(p, 0, back), a_send.at[p, 7 + back], a_recv.at[p, 7 + back],
            (y_dev, z),
        )

    def relay_y(p, back):
        return remote(
            shard(p, 1, back, 0), shard(p, 1, back, 0), a_send.at[p, 11 + back],
            a_recv.at[p, 11 + back], (y_dev, z),
        )

    def relay_x(p, back):
        return remote(
            shard(p, 2, back, 1), shard(p, 2, back, 1), a_send.at[p, 15 + back],
            a_recv.at[p, 15 + back], (x_dev, z),
        )

    def to_core(p, kind, back):
        sem = 19 + 4 * kind + back
        return remote(
            shard(p, kind, back), shard(p, kind, back), a_send.at[p, sem], a_recv.at[p, sem],
            (across, z),
        )

    half_wide = own_wide.shape[1] // 2
    parts = []
    for own, everything, cols in (
        (own_mid, all_mid, None), (own_thin, all_thin, None),
        (own_wide, all_wide, (0, half_wide)), (own_wide, all_wide, (half_wide, half_wide)),
    ):
        if cols is None:
            parts.append((own, lambda d, ref=everything: ref.at[d]))
        else:
            parts.append(
                (own.at[:, pl.ds(*cols)], lambda d, ref=everything, c=cols: ref.at[d, :, pl.ds(*c)])
            )
    chunks = ((0, 1), (2,), (3,))

    def first_far(a):
        return remote(
            parts[a][0], parts[a][1](dp), e_send.at[a, 0], e_recv.at[a, core],
            (dp - core + home, far),
        )

    def first_across(a):
        return remote(
            parts[a][0], parts[a][1](dp), e_send.at[a, 1], e_recv.at[a, core], (across, z)
        )

    def first_keep(a):
        return pltpu.make_async_copy(parts[a][0], parts[a][1](dp), e_recv.at[a, core])

    def first_arrival(a, i):
        view = parts[a][1](dp - core + i)
        return remote(view, view, e_send.at[a, 0], e_recv.at[a, i], (dp, far))

    def expert_hop(a, column, i, sem, device):
        view = parts[a][1](column - core + i)
        return remote(view, view, e_send.at[a, sem], e_recv.at[a, sem], (device, z))

    def expert_x(a, i):
        return expert_hop(a, dp, i, 2 + i, x_dev)

    def expert_y(a, i):
        return expert_hop(a, dp, i, 4 + i, y_dev)

    def expert_relay_y(a):
        return expert_hop(a, x_dev, 0, 6, y_dev)

    def expert_relay_x(a):
        return expert_hop(a, y_dev, 1, 7, x_dev)

    def expert_first(c):
        for a in chunks[c]:
            first_far(a).start()

            @pl.when(core == home)
            def _(a=a):
                first_keep(a).start()

            @pl.when(core != home)
            def _(a=a):
                first_across(a).start()

    def at_home(step, *args):
        @pl.when(core == home)
        def _():
            step(*args)

    def abroad(step, *args):
        @pl.when(core != home)
        def _():
            step(*args)

    def send_sides(a):
        for i in range(2):
            expert_x(a, i).start()
            expert_y(a, i).start()

    def spread_home(c):
        for a in chunks[c]:
            first_keep(a).wait()
            first_arrival(a, 1 - core).wait_recv()
            send_sides(a)

    def spread_far(c):
        for a in chunks[c]:
            for i in range(2):
                first_arrival(a, i).wait_recv()
            send_sides(a)

    def expert_relay(c):
        for a in chunks[c]:
            for i in range(2):
                expert_hop(a, x_dev, i, 2 + i, x_dev).wait_recv()
            expert_relay_y(a).start()
            for i in range(2):
                expert_hop(a, y_dev, i, 4 + i, y_dev).wait_recv()
            expert_relay_x(a).start()

    def expert_finish(c):
        for a in chunks[c]:
            expert_hop(a, diag, 0, 6, y_dev).wait_recv()
            expert_hop(a, diag, 1, 7, x_dev).wait_recv()
            first_far(a).wait_send()

            @pl.when(core != home)
            def _(a=a):
                first_across(a).wait_send()

            for i in range(2):
                expert_x(a, i).wait_send()
                expert_y(a, i).wait_send()
            expert_relay_y(a).wait_send()
            expert_relay_x(a).wait_send()

    gu_rows, up_rows, dn_rows = in_gu.shape[1], in_b_gu.shape[1], in_dn.shape[1]
    own_loads = [
        pltpu.make_async_copy(source.at[0], target.at[pl.ds(at_row, rows)], own_sems.at[i])
        for i, (source, target, at_row, rows) in enumerate((
            (in_gu, own_wide, 0, gu_rows), (in_b_gu, own_wide, gu_rows, up_rows),
            (in_dn, own_mid, 0, dn_rows), (in_b_dn, own_mid, dn_rows, up_rows),
            (in_a_gu, own_thin, 0, gu_rows), (in_a_dn, own_thin, gu_rows, dn_rows),
        ))
    ]
    for load in own_loads:
        load.start()
    for gathered, weight, adapter_in, adapter_out in (
        (g_qkv, in_qkv, in_a_qkv, in_b_qkv), (g_out, in_out, in_a_out, in_b_out),
    ):
        spare = gathered.shape[1] - a_rows - b_rows
        wide_cols = weight.shape[1]
        gathered[at(0, 0), :, :wide_cols] = jnp.concatenate(
            [weight[...].astype(F32), adapter_out[...].astype(F32), jnp.zeros((spare, wide_cols), F32)],
            axis=0,
        ).astype(BF16)
        gathered[at(0, 0), :, wide_cols:] = jnp.concatenate(
            [adapter_in[...].astype(F32), jnp.zeros((spare + b_rows, LANES), F32)], axis=0
        ).astype(BF16)
    next_z = z + 1 - 2 * (z % 2)
    peers = [(x_dev, z), (y_dev, z), (across, z), (across, far), (across, next_z)]
    peers += [(dp, (z + j) % 4) for j in (1, 2, 3)]
    start_kernel(None, [(device, None) for device in peers], len(peers))
    def send_own(p):
        z_sends(p, 0, lambda copy: copy.start())
        to_x(p, 0).start()
        to_y(p, 0).start()
        to_core(p, 0, 0).start()

    send_own(0)
    router[...] = jnp.concatenate(
        [router_in[...].astype(F32), jnp.zeros((CONST_LANE - kinds, MODEL_WIDTH), F32),
         const_in[...].astype(F32), jnp.zeros((LANES - CONST_LANE - 4, MODEL_WIDTH), F32)],
        axis=0,
    ).astype(BF16)
    small_s[...] = jnp.zeros_like(small_s)
    carry_parts = split_three(carry[...])
    choices_low = choices[...].astype(F32).astype(BF16)
    half_dim = HEAD_DIM // 2
    freq = jnp.exp(
        (iota((1, LANES), 1) % half_dim).astype(F32) * (-math.log(10000.0) / half_dim)
    )
    sign = jnp.where(iota((1, LANES), 1) % HEAD_DIM < half_dim, -1.0, 1.0)

    def block_rows(b):
        return pl.ds(pl.multiple_of(b * ROW_BLOCK, ROW_BLOCK), ROW_BLOCK)

    def arrange(b, carry_on):
        rows = block_rows(b)
        perm = hot_matrix(place_row[...] == b * ROW_BLOCK + iota((ROW_BLOCK, tok), 0))
        hid = dot(perm, hidden[...])
        hid_s[rows, :] = hid.astype(BF16)
        act_one[rows, :] = normed(hid, gain_one)
        return carry_on

    def arrange_rest(b, carry_on):
        rows = block_rows(b)
        perm = hot_matrix(place_row[...] == b * ROW_BLOCK + iota((ROW_BLOCK, tok), 0))
        dy_s[rows, :] = dot(perm, upstream[...]).astype(BF16)
        top, mid, last = carry_parts
        small_s[rows, :kinds] = dot_nt(perm, top) + (dot_nt(perm, mid) + dot_nt(perm, last))
        small_s[rows, CHOICE_LANE : CHOICE_LANE + 2] = dot_nt(perm, choices_low)
        return carry_on

    place = iota((1, tok), 1)
    begin_row = jnp.zeros((1, tok), jnp.int32)
    begin = 0
    for n in range(1, lengths.shape[1]):
        begin = begin + lengths[0, n - 1]
        begin_row = jnp.where(place >= begin, begin, begin_row)
    starts[...] = begin_row

    def positions(b, carry_on):
        rows = block_rows(b)
        stream = b * ROW_BLOCK + iota((ROW_BLOCK, 1), 0)
        start = jnp.zeros((ROW_BLOCK, 1), jnp.int32)
        adapter = start + adapters[0, 0]
        begin = 0
        for n in range(1, lengths.shape[1]):
            begin = begin + lengths[0, n - 1]
            start = jnp.where(stream >= begin, begin, start)
            adapter = jnp.where(stream >= begin, adapters[0, n], adapter)
        mask[rows, :] = hot_matrix(iota((ROW_BLOCK, LANES), 1) // ADAPTER_RANK == adapter)
        angle = (stream - start).astype(F32) * freq
        cosine[rows, :] = jnp.cos(angle)
        sine[rows, :] = jnp.sin(angle) * sign
        return carry_on

    lax.fori_loop(0, blocks, arrange, 0)

    at_end = (z == 0) | (z == 3)
    order = (
        jnp.where(z == 0, 3, 1), jnp.where(at_end, 2, 3),
        jnp.where(z == 0, 1, jnp.where(z == 3, 3, 2)),
    )

    def spread_shard(p, back):
        view = shard(p, 0, back)
        remote(view, view, z_send.at[p, 0], a_recv.at[p, back - 1], (dp, z)).wait_recv()
        to_x(p, back).start()
        to_y(p, back).start()
        to_core(p, 0, back).start()

    def from_z(p, t):
        @pl.when(z > t)
        def _():
            spread_shard(p, 1 + t)

        @pl.when(z + t < 3)
        def _():
            spread_shard(p, 3 - t)

        if t < 2:
            z_sends(p, t + 1, lambda copy: copy.start())

    def from_sides(p, back):
        view = shard(p, 1, back)
        remote(view, view, a_send.at[p, 3 + back], a_recv.at[p, 3 + back], (x_dev, z)).wait_recv()
        relay_y(p, back).start()
        to_core(p, 1, back).start()
        view = shard(p, 2, back)
        remote(view, view, a_send.at[p, 7 + back], a_recv.at[p, 7 + back], (y_dev, z)).wait_recv()
        relay_x(p, back).start()
        to_core(p, 2, back).start()

    def from_diag(p, back):
        view = shard(p, 3, back, 0)
        remote(view, view, a_send.at[p, 11 + back], a_recv.at[p, 11 + back], (y_dev, z)).wait_recv()
        view = shard(p, 3, back, 1)
        remote(view, view, a_send.at[p, 15 + back], a_recv.at[p, 15 + back], (x_dev, z)).wait_recv()
        to_core(p, 3, back).start()

    for t in range(3):
        from_z(0, t)
    send_own(1)
    from_sides(0, 0)
    lax.fori_loop(0, 2, arrange_rest, 0)
    from_sides(0, order[0])
    lax.fori_loop(2, 4, arrange_rest, 0)
    from_sides(0, order[1])
    lax.fori_loop(4, blocks, arrange_rest, 0)
    from_sides(0, order[2])
    for t in range(3):
        from_z(1, t)
    for load in own_loads:
        load.wait()
    for c in range(len(chunks)):
        expert_first(c)
    for back in (0,) + order[:2]:
        from_diag(0, back)
    lax.fori_loop(0, blocks, positions, 0)
    from_diag(0, order[2])
    core_columns = (across, x_dev + across - dp, y_dev + across - dp, diag + across - dp)

    def from_core(p):
        def body(back, carry):
            for kind in range(4):
                view = packs[p].at[core_columns[kind] * 4 + (z + 4 - back) % 4]
                sem = 19 + 4 * kind + back
                remote(view, view, a_send.at[p, sem], a_recv.at[p, sem], (across, z)).wait_recv()
            return carry

        lax.fori_loop(0, 4, body, 0)

    width = MODEL_WIDTH
    total = g_qkv.shape[0]

    def lay_rows(i, carry, gathered, targets):
        pair = [gathered[2 * i + n, :a_rows, :].astype(F32) for n in range(2)]
        both = jnp.concatenate(pair, axis=0).astype(BF16)
        rows = pl.ds(pl.multiple_of(i * 2 * a_rows, 16), 2 * a_rows)
        start = 0
        for target in targets:
            target[rows, :] = both[:, start : start + target.shape[1]]
            start += target.shape[1]
        return carry

    def lay_ups(i, carry, gathered, target):
        group = 16 // b_rows
        pieces = [
            gathered[group * i + n, a_rows : a_rows + b_rows, : target.shape[1]].astype(F32)
            for n in range(group)
        ]
        rows = pl.ds(pl.multiple_of(i * 16, 16), 16)
        target[rows, :] = jnp.concatenate(pieces, axis=0).astype(BF16)
        return carry

    def lay(gathered, targets, ups):
        lax.fori_loop(
            0, total // 2, functools.partial(lay_rows, gathered=gathered, targets=targets), 0
        )
        lax.fori_loop(
            0, total * b_rows // 16, functools.partial(lay_ups, gathered=gathered, target=ups), 0
        )

    def flush(first, last):
        return [
            pltpu.make_async_copy(kept[i], outs[i], out_sems.at[i]) for i in range(first, last)
        ]

    for back in (0,) + order:
        from_sides(1, back)
    for c in range(len(chunks)):
        at_home(spread_home, c)
    from_core(0)
    lay(g_qkv, (w_qkv, a_qkv), b_qkv)

    def projection(b, carry):
        rows = block_rows(b)
        low_qkv[rows, :], query[rows, :], key[rows, :], value[rows, :] = project(
            act_one[rows, :], mask[rows, :], cosine[rows, :], sine[rows, :], w_qkv, a_qkv, b_qkv
        )

        return carry

    lax.fori_loop(0, blocks, projection, 0)
    abroad(spread_far, 0)
    for copy in flush(0, 16):
        copy.start()
    lse[...] = jnp.zeros_like(lse)

    def attention(pair, carry):
        cols = pl.ds(pl.multiple_of(pair * LANES, LANES), LANES)
        attention_fwd_pair(
            pair, query.at[:, cols], key.at[:, cols], value.at[:, cols], starts,
            attn_low.at[:, cols], lse,
        )

        @pl.when(pair == 0)
        def _():
            for back in (0,) + order:
                from_diag(1, back)
            at_home(expert_relay, 0)

        @pl.when(pair == 2)
        def _():
            at_home(expert_relay, 1)

        @pl.when(pair == 3)
        def _():
            abroad(spread_far, 1)
            abroad(expert_relay, 0)

        @pl.when(pair == 4)
        def _():
            at_home(expert_relay, 2)

        return carry

    lax.fori_loop(0, HEAD_COUNT // 2, attention, 0)
    from_core(1)
    lay(g_out, (w_out, a_out), b_out)
    for copy in flush(16, 21):
        copy.start()

    def after(b, carry):
        rows = block_rows(b)
        low_out[rows, :], resid[rows, :], act_two[rows, :], gate[rows, :] = post_attn(
            kinds, attn_low[rows, :], hid_s[rows, :], mask[rows, :], small_s[rows, :],
            w_out, a_out, b_out, router, gain_two,
        )
        return carry

    lax.fori_loop(0, blocks, after, 0)
    abroad(spread_far, 2)
    abroad(expert_relay, 1)
    place_slots(4, small_s, slot, slot_rows)
    for copy in flush(21, FRONT_KEPT):
        copy.start()

    def rows_out(k):
        device = ((dp, next_z), (across, z))[k - 1]
        return remote(sent.at[k], came.at[k], row_send.at[k], row_recv.at[k], device)

    last_local = pltpu.make_async_copy(sent.at[0], last_sent, row_send.at[3])
    own_local = pltpu.make_async_copy(sent.at[0], came.at[0], row_send.at[0])
    def fill(n, carry):
        k = (n + 1) % 4
        eid = (z + k) % 2 + 2 * ((core + k // 2) % 2)
        fill_slots(eid, gate, act_two, dy_s, mask, slot_rows, sent.at[k % 3])

        @pl.when(n == 0)
        def _():
            rows_out(1).start()

        @pl.when(n == 1)
        def _():
            rows_out(2).start()

        @pl.when(n == 2)
        def _():
            last_local.start()
            last_local.wait()

        return carry

    lax.fori_loop(0, 4, fill, 0)
    own_local.start()
    abroad(expert_relay, 2)
    for c in range(len(chunks)):
        expert_finish(c)
    for k in (1, 2):
        rows_out(k).wait_recv()
        rows_out(k).wait_send()
    own_local.wait()

    def attn_sent(n, carry):
        for p in range(2):
            to_x(p, n).wait_send()
            to_y(p, n).wait_send()
            relay_x(p, n).wait_send()
            relay_y(p, n).wait_send()
            for kind in range(4):
                to_core(p, kind, n).wait_send()
        return carry

    lax.fori_loop(0, 4, attn_sent, 0)
    for p in range(2):
        for t in range(3):
            z_sends(p, t, lambda copy: copy.wait_send())
    for copy in flush(0, FRONT_KEPT):
        copy.wait()


def pair_attention_bwd_body(
    query, key, value, dout, attended, lse, starts, cosine, sine, ga_gu, gb_gu, ga_dn, gb_dn,
    d_query, d_key, d_value, own_ga_gu, own_gb_gu, own_ga_dn, own_gb_dn,
    kacc, vacc, r_ga_gu, r_gb_gu, r_ga_dn, r_gb_dn, send_sems, recv_sems,
):
    dp, z = lax.axis_index("dp"), lax.axis_index("expert")
    core, spot, half = dp % 2, dp // 2, z // 2
    own = z % 2 + 2 * core
    far = (z + 2) % 4
    at_home = core == half
    away = 1 - (core * half + (1 - core) * (1 - half))
    slot = 2 * spot + away
    groups = (
        (ga_gu, r_ga_gu, own_ga_gu), (gb_gu, r_gb_gu, own_gb_gu),
        (ga_dn, r_ga_dn, own_ga_dn), (gb_dn, r_gb_dn, own_gb_dn),
    )
    owners = 8

    def piece(i, d):
        source, target, _ = groups[i]
        count = target.shape[1]
        return source.at[pl.ds(pl.multiple_of(d * count, 16), count)]

    def push(i, d):
        return pltpu.make_async_remote_copy(
            src_ref=piece(i, d), dst_ref=groups[i][1].at[slot], send_sem=send_sems.at[i, d],
            recv_sem=recv_sems.at[i, slot], device_id=(d, own), device_id_type=MESH_ID,
        )

    def keep(i):
        return pltpu.make_async_copy(
            piece(i, dp), groups[i][1].at[2 * spot], recv_sems.at[i, 2 * spot]
        )

    def arrival(i, s):
        return pltpu.make_async_remote_copy(
            src_ref=piece(i, 0), dst_ref=groups[i][1].at[s], send_sem=send_sems.at[i, 0],
            recv_sem=recv_sems.at[i, s], device_id=(0, own), device_id_type=MESH_ID,
        )

    @pl.when(pl.program_id(0) == 0)
    def _():
        senders = []
        for m in range(owners // 2):
            device = 2 * m + half
            senders.append(((device, z), device != dp))
            senders.append(((device, far), None))
        start_kernel(None, senders, owners - 1 + away)

        def send(d, carry):
            mine = at_home & (d == dp)

            @pl.when(mine)
            def _():
                for i in range(4):
                    keep(i).start()

            @pl.when(jnp.logical_not(mine))
            def _():
                for i in range(4):
                    push(i, d).start()

            return carry

        lax.fori_loop(0, owners, send, 0)

    attention_bwd_body(
        query, key, value, dout, attended, lse, starts, cosine, sine, d_query, d_key, d_value,
        kacc, vacc,
    )

    @pl.when(pl.program_id(0) == pl.num_programs(0) - 1)
    def _():
        def finish(s, carry):
            mine = at_home & (s == 2 * spot)

            @pl.when(mine)
            def _():
                for i in range(4):
                    keep(i).wait()

            @pl.when(jnp.logical_not(mine))
            def _():
                for i in range(4):
                    arrival(i, s).wait_recv()

            @pl.when(jnp.logical_not(at_home & (s == dp)))
            def _():
                for i in range(4):
                    push(i, s).wait_send()

            return carry

        lax.fori_loop(0, owners, finish, 0)
        for _, target, out in groups:
            total = target[0].astype(F32)
            for s in range(1, owners):
                total = total + target[s].astype(F32)
            out[...] = total


def pair_tail_body(
    place_col, d_query, d_key, d_value, low_qkv, act_one, mask, a_in, b_out, gain, ga_out, gb_out,
    d_logits, hid_hbm, resid_hbm, w_hbm, out_hbm,
    out, grad_hidden, grad_gate, own_ga_qkv, own_gb_qkv, own_ga_out, own_gb_out,
    hid_s, d_resid, w_qkv, out_s, high, lower, d_low_all, ga_sum, gb_sum,
    s_ga_qkv, s_gb_qkv, s_ga_out, s_gb_out, r_ga_qkv, r_gb_qkv, r_ga_out, r_gb_out,
    thin_out, wide_out, thin_in, wide_in, load_sems, send_sems, recv_sems, far_send, far_recv,
):
    dp, z = lax.axis_index("dp"), lax.axis_index("expert")
    others, planes = 7, 3
    tok = place_col.shape[0]
    blocks = tok // ROW_BLOCK
    loads = [
        pltpu.make_async_copy(source, target, load_sems.at[i])
        for i, (source, target) in enumerate(
            ((w_hbm, w_qkv), (hid_hbm, hid_s), (resid_hbm, d_resid), (out_hbm, out_s))
        )
    ]
    for load in loads:
        load.start()
    start_kernel(
        None,
        [(((dp + i) % 8, z), None) for i in range(1, 8)] + [((dp, (z + j) % 4), None) for j in (1, 2, 3)],
        others + planes,
    )
    ga_sum[...] = jnp.zeros_like(ga_sum)
    gb_sum[...] = jnp.zeros_like(gb_sum)
    parts = [slice(p * MODEL_WIDTH, (p + 1) * MODEL_WIDTH) for p in range(3)]
    d_refs = (d_query, d_key, d_value)

    def block_rows(b):
        return pl.ds(pl.multiple_of(b * ROW_BLOCK, ROW_BLOCK), ROW_BLOCK)

    def sums(b, carry):
        rows = block_rows(b)
        low = low_qkv[rows, :]
        d_low = jnp.zeros((ROW_BLOCK, LANES), F32)
        for cols, ref in zip(parts, d_refs):
            grad = ref[rows, :]
            d_low = d_low + dot_nt(grad, b_out[:, cols])
            gb_sum[:, cols] += dot_tn(low, grad)
        d_low = (d_low * mask[rows, :].astype(F32)).astype(BF16)
        d_low_all[rows, :] = d_low
        ga_sum[...] += dot_tn(act_one[rows, :], d_low)
        return carry

    lax.fori_loop(0, blocks, sums, 0)
    s_ga_qkv[...] = ga_sum[...].astype(BF16)
    s_gb_qkv[...] = gb_sum[...].astype(BF16)
    s_ga_out[...] = ga_out[...].astype(BF16)
    s_gb_out[...] = gb_out[...].astype(BF16)
    groups = (
        (s_ga_qkv, r_ga_qkv), (s_gb_qkv, r_gb_qkv), (s_ga_out, r_ga_out), (s_gb_out, r_gb_out),
    )

    def share(i, d):
        count = groups[i][1].shape[1]
        return groups[i][0].at[pl.ds(pl.multiple_of(d * count, 16), count)]

    def near(i, n):
        goal = (dp + n + 1) % 8
        return pltpu.make_async_remote_copy(
            src_ref=share(i, goal), dst_ref=groups[i][1].at[n], send_sem=send_sems.at[i, n],
            recv_sem=recv_sems.at[i, n], device_id=(goal, z), device_id_type=MESH_ID,
        )

    def send_near(n, carry):
        for i in range(4):
            near(i, n).start()
        return carry

    lax.fori_loop(0, others, send_near, 0)

    for load in loads[:3]:
        load.wait()

    def back(b, carry):
        rows = block_rows(b)
        d_act = dot_nt(d_low_all[rows, :], a_in[...])
        for cols, ref in zip(parts, d_refs):
            d_act = d_act + dot_nt(ref[rows, :], w_qkv[:, cols])
        hid = hid_s[rows, :].astype(F32)
        scale = lax.rsqrt(jnp.mean(hid * hid, axis=-1, keepdims=True) + EPSILON)
        weighted = d_act * gain[...].astype(F32)
        grad_hid = d_resid[rows, :] + (
            scale * weighted
            - hid * (scale * scale * scale) * jnp.mean(hid * weighted, axis=-1, keepdims=True)
        )
        top = grad_hid.astype(BF16)
        high[rows, :] = top
        lower[rows, :] = (grad_hid - top.astype(F32)).astype(BF16)
        return carry

    lax.fori_loop(0, blocks, back, 0)

    def near_done(n, carry):
        for i in range(4):
            near(i, n).wait_recv()
        return carry

    lax.fori_loop(0, others, near_done, 0)
    totals = []
    for i in range(4):
        total = share(i, dp)[...].astype(F32)
        for n in range(others):
            total = total + groups[i][1][n].astype(F32)
        totals.append(total)
    a_qkv, b_qkv, a_o, b_o = totals
    a_count, b_count = a_qkv.shape[0] // 4, b_qkv.shape[0] // 4
    for p in range(4):
        a_rows, b_rows = slice(p * a_count, (p + 1) * a_count), slice(p * b_count, (p + 1) * b_count)
        thin_out[p, :a_count, :LANES] = a_qkv[a_rows].astype(BF16)
        thin_out[p, :a_count, LANES:] = a_o[a_rows].astype(BF16)
        thin_out[p, a_count:, :] = jnp.zeros((thin_out.shape[1] - a_count, 2 * LANES), BF16)
        wide_out[p] = jnp.concatenate(
            [b_qkv[b_rows, cols] for cols in parts] + [b_o[b_rows]], axis=0
        ).astype(BF16)

    def far(i, j):
        goal = (z + j + 1) % 4
        source, target = ((thin_out, thin_in), (wide_out, wide_in))[i]
        return pltpu.make_async_remote_copy(
            src_ref=source.at[goal], dst_ref=target.at[j], send_sem=far_send.at[i, j],
            recv_sem=far_recv.at[i, j], device_id=(dp, goal), device_id_type=MESH_ID,
        )

    for j in range(planes):
        for i in range(2):
            far(i, j).start()
    loads[3].wait()

    top, mid, last = (jnp.where(iota((tok, LANES), 1) < 16, v.astype(F32), 0.0) for v in split_three(d_logits[...]))
    logit_parts = (top + pltpu.roll(mid, 16, 1) + pltpu.roll(last, 32, 1)).astype(BF16)

    def to_rows(b, carry):
        rows = block_rows(b)
        perm = hot_matrix(place_col[rows, :] == iota((ROW_BLOCK, tok), 1))
        out[rows, :] = dot(perm, out_s[...]).astype(BF16)
        grad_hidden[rows, :] = dot(perm, high[...]) + dot(perm, lower[...])
        moved = dot(perm, logit_parts)
        grad_gate[rows, :] = moved + (
            pltpu.roll(moved, LANES - 16, 1) + pltpu.roll(moved, LANES - 32, 1)
        )
        return carry

    lax.fori_loop(0, blocks, to_rows, 0)
    for j in range(planes):
        for i in range(2):
            far(i, j).wait_recv()
    thin = thin_out[z].astype(F32)
    wide = wide_out[z].astype(F32)
    for j in range(planes):
        thin = thin + thin_in[j].astype(F32)
        wide = wide + wide_in[j].astype(F32)
    own_ga_qkv[...] = thin[:a_count, :LANES]
    own_ga_out[...] = thin[:a_count, LANES:]
    for p, cols in enumerate(parts):
        own_gb_qkv[:, cols] = wide[p * b_count : (p + 1) * b_count]
    own_gb_out[...] = wide[3 * b_count : 4 * b_count]

    def sent(n, carry):
        for i in range(4):
            near(i, n).wait_send()
        return carry

    lax.fori_loop(0, others, sent, 0)
    for j in range(planes):
        for i in range(2):
            far(i, j).wait_send()


def split_three(values):
    top = values.astype(BF16)
    rest = values - top.astype(F32)
    mid = rest.astype(BF16)
    return top, mid, (rest - mid.astype(F32)).astype(BF16)


def post_attn_body(
    kinds, attn_low, hid_s, mask, small_s, w_out, a_out, b_out, router, gain,
    low_out, resid, act_two, gate,
):
    low_out[...], resid[...], act_two[...], gate[...] = post_attn(
        kinds, attn_low[...], hid_s[...], mask[...], small_s[...], w_out, a_out, b_out, router, gain
    )


def post_attn(kinds, attn, hid, mask, sm, w_out, a_out, b_out, router, gain):
    low = (dot(attn, a_out[...]) * mask.astype(F32)).astype(BF16)
    res = hid.astype(F32) + (dot(attn, w_out[...]) + dot(low, b_out[...]))
    act = normed(res, gain)
    logits = dot_nt(act, router[...])
    lane = iota(logits.shape, 1)
    routed = jnp.where(lane < kinds, logits + sm, -1e30)
    top = jnp.max(routed, axis=1, keepdims=True)
    expo = jnp.exp(routed - top)
    prob = expo / jnp.sum(expo, axis=1, keepdims=True)
    return low, res, act, jnp.where(lane < kinds, prob, logits)


def place_slots(experts, small_s, slot, slot_rows):
    tok = slot.shape[0]
    lane = iota((tok, LANES), 1)
    first = small_s[:, CHOICE_LANE : CHOICE_LANE + 1].astype(jnp.int32)
    second = small_s[:, CHOICE_LANE + 1 : CHOICE_LANE + 2].astype(jnp.int32)
    hot = ((first == lane) | (second == lane)) & (lane < experts)
    hot_low = hot_matrix(hot)
    for blk in range(tok // ROW_BLOCK):
        lo, hi = blk * ROW_BLOCK, (blk + 1) * ROW_BLOCK
        tri = hot_matrix(iota((ROW_BLOCK, hi), 1) < lo + iota((ROW_BLOCK, hi), 0))
        rank = dot(tri, hot_low[:hi, :])
        slot[lo:hi, :] = jnp.where(hot[lo:hi, :], rank, -1.0)
    slot_rows[...] = slot[...].T


def fill_slots(eid, gate, act_two, dy_s, mask, slot_rows, target):
    row = slot_rows[pl.ds(eid, 1), :].astype(jnp.int32)
    pick = hot_matrix(row == iota((target.shape[0], row.shape[1]), 0))
    value = lane_value(gate[...], eid)
    scaled = (dy_s[...].astype(F32) * value).astype(BF16)
    target[:, :MODEL_WIDTH] = dot(pick, act_two[...]).astype(BF16)
    target[:, MODEL_WIDTH : 2 * MODEL_WIDTH] = dot(pick, scaled).astype(BF16)
    target[:, 2 * MODEL_WIDTH :] = dot(pick, mask[...]).astype(BF16)


def dispatch_body(experts, eids, small_s, gate, act_two, dy_s, mask, slot, sent, slot_rows):
    step = pl.program_id(0)

    @pl.when(step == 0)
    def _():
        place_slots(experts, small_s, slot, slot_rows)

    fill_slots(eids[step], gate, act_two, dy_s, mask, slot_rows, sent.at[0])


def ffn_math(
    rows, d_out, mask, w_gu, w_dn, a_gu, b_gu, a_dn, b_dn,
    ga_gu, gb_gu, ga_dn, gb_dn, acc_out, acc_dx, acc_low, acc_dlow,
):
    low_gu = (dot(rows, a_gu[...]) * mask).astype(BF16)
    dlow_dn = (dot_nt(d_out, b_dn[...]) * mask).astype(BF16)
    for ref in (acc_out, acc_dx, acc_low, acc_dlow):
        ref[...] = jnp.zeros_like(ref)

    def step(j, carry):
        lo = pl.multiple_of(j * HIDDEN_BLOCK, HIDDEN_BLOCK)
        g_cols = pl.ds(lo, HIDDEN_BLOCK)
        u_cols = pl.ds(pl.multiple_of(FEEDFWD_WIDTH + lo, HIDDEN_BLOCK), HIDDEN_BLOCK)
        gate = dot(rows, w_gu[:, g_cols]) + dot(low_gu, b_gu[:, g_cols])
        up = dot(rows, w_gu[:, u_cols]) + dot(low_gu, b_gu[:, u_cols])
        sig = 1.0 / (1.0 + jnp.exp(-gate))
        silu = gate * sig
        middle = (silu * up).astype(BF16)
        acc_out[...] += dot(middle, w_dn[g_cols, :])
        acc_low[...] += dot(middle, a_dn[g_cols, :])
        d_mid = dot_nt(d_out, w_dn[g_cols, :]) + dot_nt(dlow_dn, a_dn[g_cols, :])
        d_mid = d_mid.astype(BF16).astype(F32)
        d_gate = (d_mid * up * (sig * (1.0 + gate * (1.0 - sig)))).astype(BF16)
        d_up = (d_mid * silu).astype(BF16)
        acc_dx[...] += dot_nt(d_gate, w_gu[:, g_cols]) + dot_nt(d_up, w_gu[:, u_cols])
        acc_dlow[...] += dot_nt(d_gate, b_gu[:, g_cols]) + dot_nt(d_up, b_gu[:, u_cols])
        gb_gu[:, g_cols] += dot_tn(low_gu, d_gate)
        gb_gu[:, u_cols] += dot_tn(low_gu, d_up)
        ga_dn[g_cols, :] += dot_tn(middle, dlow_dn)
        return carry

    lax.fori_loop(0, FEEDFWD_WIDTH // HIDDEN_BLOCK, step, 0)
    low_dn = (acc_low[...] * mask).astype(BF16)
    result = (acc_out[...] + dot(low_dn, b_dn[...])).astype(BF16)
    gb_dn[...] += dot_tn(low_dn, d_out)
    dlow_gu = (acc_dlow[...] * mask).astype(BF16)
    d_rows = (acc_dx[...] + dot_nt(dlow_gu, a_gu[...])).astype(BF16)
    ga_gu[...] += dot_tn(rows, dlow_gu)
    return result, d_rows


def ffn_body(
    came, w_gu, w_dn, a_gu, b_gu, a_dn, b_dn,
    back, ga_gu, gb_gu, ga_dn, gb_dn, acc_out, acc_dx, acc_low, acc_dlow,
):
    @pl.when(pl.program_id(0) == 0)
    def _():
        for ref in (ga_gu, gb_gu, ga_dn, gb_dn):
            ref[...] = jnp.zeros_like(ref)

    back[0, :, :MODEL_WIDTH], back[0, :, MODEL_WIDTH:] = ffn_math(
        came[0, :, :MODEL_WIDTH], came[0, :, MODEL_WIDTH : 2 * MODEL_WIDTH],
        came[0, :, 2 * MODEL_WIDTH :].astype(F32), w_gu, w_dn, a_gu, b_gu, a_dn, b_dn,
        ga_gu, gb_gu, ga_dn, gb_dn, acc_out, acc_dx, acc_low, acc_dlow,
    )


def pair_ffn_body(
    had, last_sent, wide, mid, thin,
    returned, out_ga_gu, out_gb_gu, out_ga_dn, out_gb_dn,
    came, back, ga_gu, gb_gu, ga_dn, gb_dn, w_gu, w_dn, a_gu, b_gu, a_dn, b_dn, acc_out, acc_dx, acc_low, acc_dlow,
    load_sems, came_sems, back_sems, done_sems, last_sems,
):
    dp, z = lax.axis_index("dp"), lax.axis_index("expert")
    core, plane = dp % 2, z % 2

    def peer(k):
        return (dp + (k // 2) * (1 - 2 * core), z + (k % 2) * (1 - 2 * plane))

    start_kernel(None, [(peer(k), None) for k in (1, 2, 3)], 3)

    half = last_sent.shape[0] // 2
    late = pl.ds(0, 2 * half)

    def had_in(k):
        return pltpu.make_async_copy(had.at[k], came.at[k], came_sems.at[k])

    last_out = pltpu.make_async_remote_copy(
        src_ref=last_sent.at[late], dst_ref=came.at[3, late], send_sem=last_sems.at[0],
        recv_sem=last_sems.at[1], device_id=peer(3), device_id_type=MESH_ID,
    )

    def result_out(k):
        return pltpu.make_async_remote_copy(
            src_ref=back.at[k], dst_ref=returned.at[k], send_sem=back_sems.at[k],
            recv_sem=done_sems.at[k], device_id=peer(k), device_id_type=MESH_ID,
        )

    last_out.start()
    for k in (1, 0, 2):
        had_in(k).start()

    gu_rows = w_gu.shape[0] // wide.shape[0]
    up_rows = b_gu.shape[0] // wide.shape[0]
    dn_rows = w_dn.shape[0] // wide.shape[0]
    plans = (
        (wide, 0, gu_rows, w_gu), (wide, gu_rows, up_rows, b_gu), (mid, 0, dn_rows, w_dn),
        (mid, dn_rows, up_rows, b_dn), (thin, 0, gu_rows, a_gu), (thin, gu_rows, dn_rows, a_dn),
    )

    def load(d, carry):
        for i, (source, at, count, target) in enumerate(plans):
            pltpu.make_async_copy(
                source.at[d, pl.ds(at, count)],
                target.at[pl.ds(pl.multiple_of(d * count, 16), count)],
                load_sems.at[i],
            ).start()
        return carry

    lax.fori_loop(0, wide.shape[0], load, 0)
    for ref in (ga_gu, gb_gu, ga_dn, gb_dn):
        ref[...] = jnp.zeros_like(ref)
    for i, (_, _, _, target) in enumerate(plans):
        pltpu.make_async_copy(target, target, load_sems.at[i]).wait()

    def source_step(s, carry):
        k = s + 1 - 2 * (s % 2)

        @pl.when(k != 3)
        def _():
            had_in(k).wait()

        @pl.when(k == 3)
        def _():
            last_out.wait_recv()

        back[k, :, :MODEL_WIDTH], back[k, :, MODEL_WIDTH:] = ffn_math(
            came[k, :, :MODEL_WIDTH], came[k, :, MODEL_WIDTH : 2 * MODEL_WIDTH],
            came[k, :, 2 * MODEL_WIDTH :].astype(F32), w_gu, w_dn, a_gu, b_gu, a_dn, b_dn,
            ga_gu, gb_gu, ga_dn, gb_dn, acc_out, acc_dx, acc_low, acc_dlow,
        )

        @pl.when(k != 0)
        def _():
            result_out(k).start()

        return carry

    lax.fori_loop(0, 4, source_step, 0)
    for out, total in (
        (out_ga_gu, ga_gu), (out_gb_gu, gb_gu), (out_ga_dn, ga_dn), (out_gb_dn, gb_dn),
    ):
        out[...] = total[...].astype(BF16)
    own_out = pltpu.make_async_copy(back.at[0], returned.at[0], done_sems.at[0])
    own_out.start()
    own_out.wait()
    last_out.wait_send()
    for k in (1, 2, 3):
        result_out(k).wait_send()
        result_out(k).wait_recv()


def combine_body(
    experts, kinds, eids, resid, act_two, dy_s, gate, slot, small_s, low_out, attn_low, mask, came,
    w_out, a_out, b_out, router, const_value, gain,
    out_s, d_resid, d_attended, d_logits, ga_out, gb_out,
):
    @pl.when(pl.program_id(0) == 0)
    def _():
        ga_out[...] = jnp.zeros_like(ga_out)
        gb_out[...] = jnp.zeros_like(gb_out)

    rows = resid.shape[0]
    cap = came.shape[1]
    res = resid[...]
    act = act_two[...].astype(F32)
    dy_low = dy_s[...]
    dy = dy_low.astype(F32)
    lane = iota((rows, LANES), 1)
    levels = gate[...].T
    top = iota((CHOICE_ROWS, rows), 0)
    prob = jnp.where(top < kinds, levels[:CHOICE_ROWS], 0.0)

    def row(values, index):
        return jnp.sum(jnp.where(top == index, values, 0.0), axis=0, keepdims=True)

    picked = small_s[...].T
    first = picked[CHOICE_LANE : CHOICE_LANE + 1]
    second = picked[CHOICE_LANE + 1 : CHOICE_LANE + 2]

    def chosen(kind):
        return jnp.where((first == kind) | (second == kind), 1.0, 0.0)

    has_copy, has_zero, has_one = chosen(experts + 1), chosen(experts + 2), chosen(experts + 3)
    g_copy = has_copy * row(prob, experts + 1)
    g_zero = has_zero * row(prob, experts + 2)
    g_one = has_one * row(prob, experts + 3)

    def pair(at):
        left, right = levels[at : at + 1], levels[at + 1 : at + 2]
        high = jnp.maximum(left, right)
        e_left, e_right = jnp.exp(left - high), jnp.exp(right - high)
        scale = 1.0 / (e_left + e_right)
        return e_left * scale, e_right * scale

    a00, a01 = pair(CONST_LANE)
    a10, a11 = pair(CONST_LANE + 2)
    coef = g_copy + g_zero * a00 + g_one * a10
    factors = [coef, g_zero * a01, g_one * a11]
    factors += [row(prob, eids[k]) for k in range(came.shape[0])]
    spot = iota((LANES, rows), 0)
    columns = jnp.zeros((LANES, rows), F32)
    for n, factor in enumerate(factors):
        columns = jnp.where(spot == n, factor, columns)
    columns = columns.T
    v_zero, v_one = const_value[0:1, :], const_value[1:2, :]
    out = res + columns[:, 0:1] * act + columns[:, 1:2] * v_zero + columns[:, 2:3] * v_one
    d_act = columns[:, 0:1] * dy
    met = jnp.where(lane == 0, jnp.sum(dy * act, axis=1, keepdims=True), 0.0)
    met = jnp.where(lane == 1, jnp.sum(dy * v_zero, axis=1, keepdims=True), met)
    met = jnp.where(lane == 2, jnp.sum(dy * v_one, axis=1, keepdims=True), met)
    for k in range(came.shape[0]):
        place = lane_value(slot[...], eids[k]).astype(jnp.int32)
        pick = hot_matrix(place == iota((rows, cap), 1))
        result = dot(pick, came[k, :, :MODEL_WIDTH])
        d_act = d_act + dot(pick, came[k, :, MODEL_WIDTH:])
        met = jnp.where(lane == 3 + k, jnp.sum(dy * result, axis=1, keepdims=True), met)
        out = out + columns[:, 3 + k : 4 + k] * result
    out_s[...] = out.astype(BF16)
    met = met.T
    along_act, along_zero, along_one = met[0:1], met[1:2], met[2:3]
    d_gate = jnp.zeros((CHOICE_ROWS, rows), F32)
    for k in range(came.shape[0]):
        d_gate = jnp.where(top == eids[k], met[3 + k : 4 + k], d_gate)
    d_gate = jnp.where(top == experts + 1, has_copy * along_act, d_gate)
    d_gate = jnp.where(top == experts + 2, has_zero * (a00 * along_act + a01 * along_zero), d_gate)
    d_gate = jnp.where(top == experts + 3, has_one * (a10 * along_act + a11 * along_one), d_gate)
    d_logit = prob * (d_gate - jnp.sum(prob * d_gate, axis=0, keepdims=True))
    tail = iota((8, rows), 0)
    d_pair = jnp.zeros((8, rows), F32)
    for n, (g_val, left, right, along) in enumerate(
        ((g_zero, a00, a01, along_zero), (g_one, a10, a11, along_one))
    ):
        da_left, da_right = g_val * along_act, g_val * along
        level = left * da_left + right * da_right
        d_pair = jnp.where(tail == 2 * n, left * (da_left - level), d_pair)
        d_pair = jnp.where(tail == 2 * n + 1, right * (da_right - level), d_pair)
    mix = jnp.concatenate(
        [d_logit, jnp.zeros((CONST_LANE - CHOICE_ROWS, rows), F32), d_pair,
         jnp.zeros((LANES - CONST_LANE - 8, rows), F32)],
        axis=0,
    ).T
    d_logits[...] = mix
    mix_hi = mix.astype(BF16)
    mix_lo = (mix - mix_hi.astype(F32)).astype(BF16)
    d_act = d_act + (dot(mix_hi, router[...]) + dot(mix_lo, router[...]))
    scale = lax.rsqrt(jnp.mean(res * res, axis=-1, keepdims=True) + EPSILON)
    weighted = d_act * gain[...].astype(F32)
    d_res = dy + (
        scale * weighted
        - res * (scale * scale * scale) * jnp.mean(res * weighted, axis=-1, keepdims=True)
    )
    d_resid[...] = d_res
    d_attn = d_res.astype(BF16)
    dlow = (dot_nt(d_attn, b_out[...]) * mask[...].astype(F32)).astype(BF16)
    gb_out[...] += dot_tn(low_out[...], d_attn)
    ga_out[...] += dot_tn(attn_low[...], dlow)
    d_attended[...] = (dot_nt(d_attn, w_out[...]) + dot_nt(dlow, a_out[...])).astype(BF16)


def input_grad_body(
    d_query, d_key, d_value, low_qkv, act_one, mask, hid_s, d_resid, w_qkv, a_in, b_out, gain,
    high, lower, ga_qkv, gb_qkv,
):
    @pl.when(pl.program_id(0) == 0)
    def _():
        ga_qkv[...] = jnp.zeros_like(ga_qkv)
        gb_qkv[...] = jnp.zeros_like(gb_qkv)

    d_low = jnp.zeros((d_query.shape[0], LANES), F32)
    d_act = jnp.zeros((d_query.shape[0], MODEL_WIDTH), F32)
    for part, ref in enumerate((d_query, d_key, d_value)):
        cols = slice(part * MODEL_WIDTH, (part + 1) * MODEL_WIDTH)
        grad = ref[...]
        d_low = d_low + dot_nt(grad, b_out[:, cols])
        d_act = d_act + dot_nt(grad, w_qkv[:, cols])
        gb_qkv[:, cols] += dot_tn(low_qkv[...], grad)
    d_low = (d_low * mask[...].astype(F32)).astype(BF16)
    ga_qkv[...] += dot_tn(act_one[...], d_low)
    d_act = d_act + dot_nt(d_low, a_in[...])
    hid = hid_s[...].astype(F32)
    scale = lax.rsqrt(jnp.mean(hid * hid, axis=-1, keepdims=True) + EPSILON)
    weighted = d_act * gain[...].astype(F32)
    grad_hid = d_resid[...] + (
        scale * weighted
        - hid * (scale * scale * scale) * jnp.mean(hid * weighted, axis=-1, keepdims=True)
    )
    top = grad_hid.astype(BF16)
    high[...] = top
    lower[...] = (grad_hid - top.astype(F32)).astype(BF16)


def to_rows_body(place_col, out_s, d_logits, high, lower, out, grad_hidden, grad_gate):
    rows = out.shape[0]
    tok = out_s.shape[0]
    perm = hot_matrix(place_col[...] == iota((rows, tok), 1))
    out[...] = dot(perm, out_s[...]).astype(BF16)
    grad_hidden[...] = dot(perm, high[...]) + dot(perm, lower[...])
    logits = d_logits[...]
    top = logits.astype(BF16)
    rest = logits - top.astype(F32)
    mid = rest.astype(BF16)
    last = (rest - mid.astype(F32)).astype(BF16)
    grad_gate[...] = dot(perm, top) + (dot(perm, mid) + dot(perm, last))


class PairPlan:
    paired = True

    def __init__(self, dp, ex):
        self.ex = ex

    def expert_ids(self):
        own = lax.axis_index("expert") % 2 + 2 * (lax.axis_index("dp") % 2)
        return own ^ jnp.arange(self.ex, dtype=jnp.int32)


class AxisPlan:
    paired = False

    def __init__(self, dp, ex):
        self.dp, self.ex = dp, ex

    def gather(self, shard):
        return lax.all_gather(shard, "dp", axis=0)

    def expert_ids(self):
        return jnp.arange(self.ex, dtype=jnp.int32)

    def exchange(self, values):
        return lax.all_to_all(values, "expert", split_axis=0, concat_axis=0, tiled=True)

    def reduce(self, sums):
        return lax.psum_scatter(sums, "dp", scatter_dimension=0, tiled=True)[0].astype(F32)

    def reduce_all(self, sums):
        return lax.psum_scatter(
            sums, ("dp", "expert"), scatter_dimension=0, tiled=True
        )[0].astype(F32)


def shards(
    dp_size,
    expert_count,
    hidden_input,
    gate_carryover,
    sequence_length,
    token_stream_place,
    expert_choice_index,
    sequence_adapter,
    attention_gain,
    query_key_weight,
    output_weight,
    adapter_in_query,
    adapter_out_query,
    adapter_in_output,
    adapter_out_output,
    feedfwd_gain,
    router_weight,
    constant_gate,
    constant_value,
    gate_upward_weight,
    down_weight,
    adapter_in_gate,
    adapter_out_gate,
    adapter_in_down,
    adapter_out_down,
    output_gradient,
):
    tok = hidden_input.shape[0]
    width = MODEL_WIDTH
    kinds = expert_count + 4
    devices = dp_size * expert_count
    capacity = 5 * tok // (2 * kinds) // 8 * 8 + 8
    cap = -(-capacity // 16) * 16
    blocks = tok // ROW_BLOCK
    plan = (PairPlan if (dp_size, expert_count) == (8, 4) else AxisPlan)(dp_size, expert_count)

    a_rows, b_rows = query_key_weight.shape[0], adapter_out_query.shape[0]
    gu_rows, up_rows, dn_rows = (
        gate_upward_weight.shape[1], adapter_out_gate.shape[1], down_weight.shape[1],
    )
    gain_one, gain_two = attention_gain[None, :], feedfwd_gain[None, :]
    const_value = constant_value.astype(F32)
    sent_width = 2 * width + LANES
    full = whole
    hbm = pl.BlockSpec(memory_space=pl.ANY)
    vmem = pl.BlockSpec(memory_space=pltpu.VMEM)
    pairs = HEAD_COUNT // 2
    lse_rows = -(-HEAD_COUNT // 8) * 8
    smem = pl.BlockSpec(memory_space=pltpu.SMEM)
    eids = plan.expert_ids()
    if plan.paired:
        shapes = [
            sds((tok, width), BF16), sds((tok, width), BF16), sds((tok, LANES), F32),
            sds((tok, width), BF16), sds((tok, LANES), BF16), sds((tok, LANES), BF16),
            sds((1, tok), jnp.int32), sds((tok, LANES), F32), sds((tok, LANES), F32),
            sds((LANES, width), BF16),
            sds((tok, width), BF16), sds((tok, width), BF16), sds((tok, width), BF16),
            sds((width, 3 * width), BF16), sds((width, LANES), BF16), sds((LANES, 3 * width), BF16),
            sds((width, width), BF16), sds((width, LANES), BF16), sds((LANES, width), BF16),
            sds((tok, width), BF16), sds((lse_rows, tok), F32), sds((tok, LANES), BF16),
            sds((tok, width), F32), sds((tok, width), BF16), sds((tok, LANES), F32),
            sds((tok, LANES), F32),
        ]
        shard_rows = -(-(a_rows + b_rows) // 16) * 16
        packed = [
            (gu_rows + up_rows, 2 * FEEDFWD_WIDTH), (dn_rows + up_rows, width),
            (gu_rows + dn_rows, LANES),
        ]
        row_shape = (expert_count, cap, sent_width)
        (
            hid_s, dy_s, small_s, act_one, low_qkv, mask, starts, cosine, sine, router,
            query, key, value, w_qkv, a_qkv, b_qkv, w_out, a_out, b_out,
            attn_low, lse, low_out, resid, act_two, gate, slot,
            wide, mid, thin, came, last_sent,
        ) = pl.pallas_call(
            functools.partial(pair_front_body, kinds, a_rows, b_rows),
            in_specs=[smem] * 2 + [vmem] * 15 + [hbm] * 6,
            out_specs=[hbm] * (FRONT_KEPT + 5),
            out_shape=shapes
            + [sds((dp_size,) + shape, BF16) for shape in packed]
            + [sds(row_shape, BF16), sds(row_shape[1:], BF16)],
            scratch_shapes=[pltpu.VMEM(s.shape, s.dtype) for s in shapes]
            + [
                pltpu.VMEM((devices, shard_rows, 3 * width + LANES), BF16),
                pltpu.VMEM((devices, shard_rows, width + LANES), BF16),
                *[pltpu.VMEM(shape, BF16) for shape in packed],
                pltpu.VMEM((3,) + row_shape[1:], BF16),
                pltpu.VMEM((LANES, tok), F32),
                pltpu.SemaphoreType.DMA((2, 35)), pltpu.SemaphoreType.DMA((2, 35)),
                pltpu.SemaphoreType.DMA((2, 6)),
                pltpu.SemaphoreType.DMA((4, 8)), pltpu.SemaphoreType.DMA((4, 8)),
                pltpu.SemaphoreType.DMA((FRONT_KEPT,)), pltpu.SemaphoreType.DMA((6,)),
                pltpu.SemaphoreType.DMA((5,)), pltpu.SemaphoreType.DMA((4,)),
            ],
            compiler_params=pltpu.CompilerParams(
                vmem_limit_bytes=VMEM_BYTES, collective_id=4, has_side_effects=True
            ),
            name="pair_front",
        )(sequence_length, sequence_adapter, token_stream_place, hidden_input, output_gradient,
          gate_carryover.T, expert_choice_index.T, gain_one, gain_two, router_weight.T,
          constant_gate.T,
          query_key_weight, output_weight, adapter_in_query, adapter_in_output, adapter_out_query,
          adapter_out_output, gate_upward_weight, adapter_out_gate, down_weight, adapter_out_down,
          adapter_in_gate, adapter_in_down)
        place = token_stream_place[0]
    else:
        pad_rows = -(a_rows + b_rows) % 16

        def pack(weight, adapter_in, adapter_out):
            lower = jnp.pad(adapter_out, ((0, pad_rows), (0, LANES)))
            return jnp.concatenate([jnp.concatenate([weight, adapter_in], axis=1), lower], axis=0)

        own_qkv = pack(query_key_weight, adapter_in_query, adapter_out_query)
        own_out = pack(output_weight, adapter_in_output, adapter_out_output)
        own_wide = jnp.concatenate([gate_upward_weight[0], adapter_out_gate[0]], axis=0)
        own_mid = jnp.concatenate([down_weight[0], adapter_out_down[0]], axis=0)
        own_thin = jnp.concatenate([adapter_in_gate[0], adapter_in_down[0]], axis=0)

        place = token_stream_place[0]
        ends = jnp.cumsum(sequence_length[0])
        begins = ends - sequence_length[0]
        stream = jnp.arange(tok, dtype=jnp.int32)
        seg = jnp.sum((stream[:, None] >= ends[None, :]).astype(jnp.int32), axis=1)
        seg_hot = seg[:, None] == jnp.arange(ends.shape[0], dtype=jnp.int32)[None, :]
        start = jnp.sum(jnp.where(seg_hot, begins[None, :], 0), axis=1)
        adapter = jnp.sum(jnp.where(seg_hot, sequence_adapter[0][None, :], 0), axis=1)
        half = HEAD_DIM // 2
        freq = jnp.exp(jnp.arange(half, dtype=F32) * (-math.log(10000.0) / half))
        angle = (stream - start).astype(F32)[:, None] * freq[None, :]
        cos, sin = jnp.cos(angle), jnp.sin(angle)
        cosine = jnp.concatenate([cos, cos, cos, cos], axis=1)
        sine = jnp.concatenate([-sin, sin, -sin, sin], axis=1)
        starts = start[None, :]
        mask = (jnp.arange(LANES)[None, :] // ADAPTER_RANK == adapter[:, None]).astype(BF16)
        top, middle, last = split_three(gate_carryover)
        gap = jnp.zeros((tok, 16 - kinds), BF16)
        small = jnp.concatenate(
            [top, gap, middle, gap, last, gap, expert_choice_index.astype(BF16),
             jnp.zeros((tok, LANES - CHOICE_LANE - 2), BF16)],
            axis=1,
        )
        router = jnp.concatenate(
            [router_weight.T, jnp.zeros((CONST_LANE - kinds, width), BF16), constant_gate.T,
             jnp.zeros((LANES - CONST_LANE - 4, width), BF16)],
            axis=0,
        )

        all_qkv = lax.all_gather(own_qkv, ("dp", "expert"), axis=0)
        all_out = lax.all_gather(own_out, ("dp", "expert"), axis=0)
        upper = slice(a_rows, a_rows + b_rows)
        w_qkv = all_qkv[:, :a_rows, : 3 * width].reshape(width, 3 * width)
        a_qkv = all_qkv[:, :a_rows, 3 * width :].reshape(width, LANES)
        b_qkv = all_qkv[:, upper, : 3 * width].reshape(LANES, 3 * width)
        w_out = all_out[:, :a_rows, :width].reshape(width, width)
        a_out = all_out[:, :a_rows, width:].reshape(width, LANES)
        b_out = all_out[:, upper, :width].reshape(LANES, width)
        wide, mid, thin = (plan.gather(w) for w in (own_wide, own_mid, own_thin))
        hid_s, dy_s, small_s, act_one, low_qkv, query, key, value = call(
            proj_in_body,
            (blocks,),
            [full((1, tok)), full((tok, width)), full((tok, width)), full((tok, LANES)),
             row_spec(LANES), row_spec(LANES), row_spec(LANES), full((1, width)),
             full((width, 3 * width)), full((width, LANES)), full((LANES, 3 * width))],
            [row_spec(width), row_spec(width), row_spec(LANES), row_spec(width), row_spec(LANES),
             row_spec(width), row_spec(width), row_spec(width)],
            [sds((tok, width), BF16), sds((tok, width), BF16), sds((tok, LANES), F32),
             sds((tok, width), BF16), sds((tok, LANES), BF16), sds((tok, width), BF16),
             sds((tok, width), BF16), sds((tok, width), BF16)],
            name="proj_in",
        )(place[None, :], hidden_input, output_gradient, small, cosine, sine, mask, gain_one,
          w_qkv, a_qkv, b_qkv)

        attn_low, lse = call(
            attention_fwd_body,
            (pairs,),
            [col_spec(tok)] * 3 + [full((1, tok))],
            [col_spec(tok), full((lse_rows, tok))],
            [sds((tok, width), BF16), sds((lse_rows, tok), F32)],
            name="attention_fwd",
        )(query, key, value, starts)

        low_out, resid, act_two, gate = call(
            functools.partial(post_attn_body, kinds),
            (blocks,),
            [row_spec(width), row_spec(width), row_spec(LANES), row_spec(LANES), full((width, width)),
             full((width, LANES)), full((LANES, width)), full((LANES, width)), full((1, width))],
            [row_spec(LANES), row_spec(width), row_spec(width), row_spec(LANES)],
            [sds((tok, LANES), BF16), sds((tok, width), F32), sds((tok, width), BF16),
             sds((tok, LANES), F32)],
            name="post_attn",
        )(attn_low, hid_s, mask, small_s, w_out, a_out, b_out, router, gain_two)

        slot, sent = call(
            functools.partial(dispatch_body, expert_count),
            (expert_count,),
            [smem, full((tok, LANES)), full((tok, LANES)), full((tok, width)), full((tok, width)),
             full((tok, LANES))],
            [full((tok, LANES)), pl.BlockSpec((1, cap, sent_width), lambda i: (i, 0, 0))],
            [sds((tok, LANES), F32), sds((expert_count, cap, sent_width), BF16)],
            scratch=[pltpu.VMEM((LANES, tok), F32)],
            name="dispatch",
        )(eids, small_s, gate, act_two, dy_s, mask)

    grad_shapes = [
        sds((width, LANES), F32), sds((LANES, 2 * FEEDFWD_WIDTH), F32),
        sds((FEEDFWD_WIDTH, LANES), F32), sds((LANES, width), F32),
    ]
    accumulators = [
        pltpu.VMEM((cap, width), F32), pltpu.VMEM((cap, width), F32),
        pltpu.VMEM((cap, LANES), F32), pltpu.VMEM((cap, LANES), F32),
    ]
    if plan.paired:
        returned, ga_gu, gb_gu, ga_dn, gb_dn = pl.pallas_call(
            pair_ffn_body,
            in_specs=[hbm] * 5,
            out_specs=[hbm] + [vmem] * 4,
            out_shape=[sds((expert_count, cap, 2 * width), BF16)]
            + [sds(g.shape, BF16) for g in grad_shapes],
            scratch_shapes=[
                pltpu.VMEM((expert_count, cap, sent_width), BF16),
                pltpu.VMEM((expert_count, cap, 2 * width), BF16),
                *[pltpu.VMEM(g.shape, F32) for g in grad_shapes],
                pltpu.VMEM((width, 2 * FEEDFWD_WIDTH), BF16), pltpu.VMEM((FEEDFWD_WIDTH, width), BF16),
                pltpu.VMEM((width, LANES), BF16), pltpu.VMEM((LANES, 2 * FEEDFWD_WIDTH), BF16),
                pltpu.VMEM((FEEDFWD_WIDTH, LANES), BF16), pltpu.VMEM((LANES, width), BF16),
                *accumulators,
                pltpu.SemaphoreType.DMA((6,)),
                *[pltpu.SemaphoreType.DMA((expert_count,)) for _ in range(3)],
                pltpu.SemaphoreType.DMA((2,)),
            ],
            compiler_params=pltpu.CompilerParams(
                vmem_limit_bytes=VMEM_BYTES, collective_id=1, has_side_effects=True
            ),
            name="pair_ffn",
        )(came, last_sent, wide, mid, thin)
    else:
        w_gu = wide[:, :gu_rows].reshape(width, 2 * FEEDFWD_WIDTH)
        b_gu = wide[:, gu_rows:].reshape(LANES, 2 * FEEDFWD_WIDTH)
        w_dn = mid[:, :dn_rows].reshape(FEEDFWD_WIDTH, width)
        b_dn = mid[:, dn_rows:].reshape(LANES, width)
        a_gu = thin[:, :gu_rows].reshape(width, LANES)
        a_dn = thin[:, gu_rows:].reshape(FEEDFWD_WIDTH, LANES)
        came = plan.exchange(sent)
        back, ga_gu, gb_gu, ga_dn, gb_dn = call(
            ffn_body,
            (expert_count,),
            [pl.BlockSpec((1, cap, sent_width), lambda i: (i, 0, 0)),
             full((width, 2 * FEEDFWD_WIDTH)), full((FEEDFWD_WIDTH, width)), full((width, LANES)),
             full((LANES, 2 * FEEDFWD_WIDTH)), full((FEEDFWD_WIDTH, LANES)), full((LANES, width))],
            [pl.BlockSpec((1, cap, 2 * width), lambda i: (i, 0, 0)), full((width, LANES)),
             full((LANES, 2 * FEEDFWD_WIDTH)), full((FEEDFWD_WIDTH, LANES)), full((LANES, width))],
            [sds((expert_count, cap, 2 * width), BF16)] + grad_shapes,
            scratch=accumulators,
            name="ffn",
        )(came, w_gu, w_dn, a_gu, b_gu, a_dn, b_dn)
        returned = plan.exchange(back)

    out_s, d_resid, d_attended, d_logits, ga_out, gb_out = call(
        functools.partial(combine_body, expert_count, kinds),
        (tok // ROW_BLOCK,),
        [smem, row_spec(width, ROW_BLOCK), row_spec(width, ROW_BLOCK), row_spec(width, ROW_BLOCK), row_spec(LANES, ROW_BLOCK), row_spec(LANES, ROW_BLOCK),
         row_spec(LANES, ROW_BLOCK), row_spec(LANES, ROW_BLOCK), row_spec(width, ROW_BLOCK), row_spec(LANES, ROW_BLOCK),
         full((expert_count, cap, 2 * width)), full((width, width)), full((width, LANES)),
         full((LANES, width)), full((LANES, width)), full((2, width)), full((1, width))],
        [row_spec(width, ROW_BLOCK), row_spec(width, ROW_BLOCK), row_spec(width, ROW_BLOCK), row_spec(LANES, ROW_BLOCK), full((width, LANES)),
         full((LANES, width))],
        [sds((tok, width), BF16), sds((tok, width), F32), sds((tok, width), BF16),
         sds((tok, LANES), F32), sds((width, LANES), F32), sds((LANES, width), F32)],
        name="combine",
    )(eids, resid, act_two, dy_s, gate, slot, small_s, low_out, attn_low, mask, returned,
      w_out, a_out, b_out, router, const_value, gain_two)

    if plan.paired:
        flow = dict(vmem_limit_bytes=VMEM_BYTES, has_side_effects=True)
        own_shapes = [
            sds((gu_rows, LANES), F32), sds((up_rows, 2 * FEEDFWD_WIDTH), F32),
            sds((dn_rows, LANES), F32), sds((up_rows, width), F32),
        ]
        d_query, d_key, d_value, *expert_owned = pl.pallas_call(
            pair_attention_bwd_body,
            grid=(pairs,),
            in_specs=[col_spec(tok)] * 5
            + [full((lse_rows, tok)), full((1, tok)), full((tok, LANES)), full((tok, LANES))]
            + [hbm] * 4,
            out_specs=[col_spec(tok)] * 3 + [full(s.shape) for s in own_shapes],
            out_shape=[sds((tok, width), BF16)] * 3 + own_shapes,
            scratch_shapes=[pltpu.VMEM((tok, LANES), F32), pltpu.VMEM((tok, LANES), F32)]
            + [pltpu.VMEM((dp_size,) + s.shape, BF16) for s in own_shapes]
            + [pltpu.SemaphoreType.DMA((4, dp_size)), pltpu.SemaphoreType.DMA((4, dp_size))],
            compiler_params=pltpu.CompilerParams(collective_id=2, **flow),
            name="pair_attention_bwd",
        )(query, key, value, d_attended, attn_low, lse, starts, cosine, sine,
          ga_gu, gb_gu, ga_dn, gb_dn)
        sum_shapes = [(width, LANES), (LANES, 3 * width), (width, LANES), (LANES, width)]
        got_shapes = [(dp_size - 1, a // dp_size, b) for a, b in sum_shapes]
        thin_rows = -(-a_rows // 16) * 16
        output, grad_hidden, grad_gate, *attn_owned = pl.pallas_call(
            pair_tail_body,
            in_specs=[vmem] * 13 + [hbm] * 4,
            out_specs=[vmem] * 7,
            out_shape=[
                sds((tok, width), BF16), sds((tok, width), F32), sds((tok, LANES), F32),
                sds((a_rows, LANES), F32), sds((b_rows, 3 * width), F32),
                sds((a_rows, LANES), F32), sds((b_rows, width), F32),
            ],
            scratch_shapes=[
                pltpu.VMEM((tok, width), BF16), pltpu.VMEM((tok, width), F32),
                pltpu.VMEM((width, 3 * width), BF16), pltpu.VMEM((tok, width), BF16),
                pltpu.VMEM((tok, width), BF16), pltpu.VMEM((tok, width), BF16),
                pltpu.VMEM((tok, LANES), BF16),
                pltpu.VMEM((width, LANES), F32), pltpu.VMEM((LANES, 3 * width), F32),
                *[pltpu.VMEM(shape, BF16) for shape in sum_shapes + got_shapes],
                pltpu.VMEM((expert_count, thin_rows, 2 * LANES), BF16),
                pltpu.VMEM((expert_count, 4 * b_rows, width), BF16),
                pltpu.VMEM((expert_count - 1, thin_rows, 2 * LANES), BF16),
                pltpu.VMEM((expert_count - 1, 4 * b_rows, width), BF16),
                pltpu.SemaphoreType.DMA((4,)),
                pltpu.SemaphoreType.DMA((4, dp_size - 1)), pltpu.SemaphoreType.DMA((4, dp_size - 1)),
                pltpu.SemaphoreType.DMA((2, expert_count - 1)),
                pltpu.SemaphoreType.DMA((2, expert_count - 1)),
            ],
            compiler_params=pltpu.CompilerParams(collective_id=3, **flow),
            name="pair_tail",
        )(place[:, None], d_query, d_key, d_value, low_qkv, act_one, mask, a_qkv, b_qkv, gain_one,
          ga_out, gb_out, d_logits, hid_s, d_resid, w_qkv, out_s)
        return (
            output, grad_hidden, grad_gate[:, :kinds], *attn_owned,
            *[expert_owned[i][None] for i in range(4)],
        )

    owned_wide = plan.reduce(
        jnp.concatenate([gb_gu, gb_dn], axis=1).astype(BF16).reshape(dp_size, up_rows, -1)
    )
    owned_thin = plan.reduce(
        jnp.concatenate(
            [ga_gu.reshape(dp_size, gu_rows, LANES), ga_dn.reshape(dp_size, dn_rows, LANES)], axis=1
        ).astype(BF16)
    )

    d_query, d_key, d_value = call(
        attention_bwd_body,
        (pairs,),
        [col_spec(tok)] * 5
        + [full((lse_rows, tok)), full((1, tok)), full((tok, LANES)), full((tok, LANES))],
        [col_spec(tok)] * 3,
        [sds((tok, width), BF16)] * 3,
        scratch=[pltpu.VMEM((tok, LANES), F32), pltpu.VMEM((tok, LANES), F32)],
        name="attention_bwd",
    )(query, key, value, d_attended, attn_low, lse, starts, cosine, sine)

    high, lower, ga_qkv, gb_qkv = call(
        input_grad_body,
        (blocks,),
        [row_spec(width)] * 3 + [row_spec(LANES), row_spec(width), row_spec(LANES), row_spec(width),
         row_spec(width), full((width, 3 * width)), full((width, LANES)), full((LANES, 3 * width)),
         full((1, width))],
        [row_spec(width), row_spec(width), full((width, LANES)), full((LANES, 3 * width))],
        [sds((tok, width), BF16), sds((tok, width), BF16), sds((width, LANES), F32),
         sds((LANES, 3 * width), F32)],
        name="input_grad",
    )(d_query, d_key, d_value, low_qkv, act_one, mask, hid_s, d_resid, w_qkv, a_qkv, b_qkv,
      gain_one)

    owned = plan.reduce_all(
        jnp.concatenate(
            [
                ga_qkv.reshape(devices, b_rows, -1),
                ga_out.reshape(devices, b_rows, -1),
                gb_qkv.reshape(devices, b_rows, -1),
                gb_out.reshape(devices, b_rows, -1),
            ],
            axis=2,
        ).astype(BF16)
    )

    output, grad_hidden, grad_gate = call(
        to_rows_body,
        (blocks,),
        [row_spec(1), full((tok, width)), full((tok, LANES)), full((tok, width)),
         full((tok, width))],
        [row_spec(width), row_spec(width), row_spec(LANES)],
        [sds((tok, width), BF16), sds((tok, width), F32), sds((tok, LANES), F32)],
        name="to_rows",
    )(place[:, None], out_s, d_logits, high, lower)

    return (
        output,
        grad_hidden,
        grad_gate[:, :kinds],
        owned[:, :width].reshape(a_rows, LANES),
        owned[:, 2 * width : 5 * width],
        owned[:, width : 2 * width].reshape(a_rows, LANES),
        owned[:, 5 * width :],
        owned_thin[None, :gu_rows],
        owned_wide[None, :, : 2 * FEEDFWD_WIDTH],
        owned_thin[None, gu_rows:],
        owned_wide[None, :, 2 * FEEDFWD_WIDTH :],
    )


def solution(mesh):
    rows = P(("dp", "expert"), None)
    expert_rows = P("expert", "dp", None)
    in_specs = (
        (rows,) * 6 + (P(),) + (rows,) * 6 + (P(),) * 4 + (expert_rows,) * 6 + (rows,)
    )
    out_specs = (rows,) * 7 + (expert_rows,) * 4
    body = functools.partial(shards, mesh.shape["dp"], mesh.shape["expert"])
    return jax.shard_map(body, mesh=mesh, in_specs=in_specs, out_specs=out_specs, check_vma=False)
```

profile of v0, /device:TPU:1, one launch (start us, length us, event | category | flops | bytes accessed | tf_op | source)
XLA Modules:
  0.0 369.1 jit_solution(11143661059674596426)
XLA Ops:
  0.6 1.3 broadcast_in_dim.18.gain_one.gain
  1.9 1.3 broadcast_in_dim.19.gain_two.gain
  3.2 136.8 %pair_front.1 = (bf16[1280,768]{1,0:T(8,128)(2,1)}, bf16[1280,768]{1,0:T(8,128)(2,1)}, f32[1280,128]{1,0:T(8,128)}, bf16[1280,768]{1,0:T(8,128)(2,1)}, bf16[1280...) custom-call(s32[1,5]{1,0:T(1,128)} %lengths.1, ...), custom_call_target="tpu_custom_call" | custom-call | tf_op jit(solution)/shard_map/pair_front/pallas_call | solution.py:1522
  140.0 0.0 copy-start.10
  140.0 88.7 %pair_ffn.1 = (bf16[4,416,1536]{2,1,0:T(8,128)(2,1)}, bf16[768,128]{1,0:T(8,128)(2,1)}, bf16[128,4096]{1,0:T(8,128)(2,1)}, bf16[2048,128]{1,0:T(8,128)(2,1)}, bf16[128,768]{1,0:T(8,128)(2,1)}) custom-call(bf16[4,416,1664]{2,1,0:T(8,128)(2,1)} %get-tuple-element.79.had, bf16[416,1664]{1,0:T(8,128)(2,1)} %get-tuple-element.80.last_sent, ...), custom_call_target="tpu_custom_call" | custom-call | tf_op jit(solution)/shard_map/pair_ffn/pallas_call | solution.py:1660
  228.7 0.5 iota_xor_fusion.eids
  229.2 0.0 copy-done.10
  229.2 0.6 convert_element_type.3.const_value
  229.8 26.6 %combine.1 = (bf16[1280,768]{1,0:T(8,128)(2,1)}, f32[1280,768]{1,0:T(8,128)}, bf16[1280,768]{1,0:T(8,128)(2,1)}, f32[1280,128]{1,0:T(8,128)}, f32[768,128]{1,0:T(8,128)}, /*index=5*/f32[128,768]{1,0:T(8,128)}) custom-call(s32[4]{0:T(128)} %iota_xor_fusion.eids, f32[1280,768]{1,0:T(8,128)} %get-tuple-element.70.resid, ...), custom_call_target="tpu_custom_call" | custom-call | tf_op jit(solution)/shard_map/combine/pallas_call | solution.py:1705
  256.4 0.0 copy-start.6
  256.4 46.8 %pair_attention_bwd.1 = (bf16[1280,768]{1,0:T(8,128)(2,1)}, bf16[1280,768]{1,0:T(8,128)(2,1)}, bf16[1280,768]{1,0:T(8,128)(2,1)}, f32[96,128]{1,0:T(8,128)}, f32...) custom-call(bf16[1280,768]{1,0:T(8,128)(2,1)} %get-tuple-element.67.query, ...), custom_call_target="tpu_custom_call" | custom-call | tf_op jit(solution)/shard_map/pair_attention_bwd/pallas_call | solution.py:1726
  303.2 1.1 copy.36.place_col
  304.3 52.5 %pair_tail.1 = (bf16[1280,768]{1,0:T(8,128)(2,1)}, f32[1280,768]{1,0:T(8,128)}, f32[1280,128]{1,0:T(8,128)}, f32[24,128]{1,0:T(8,128)}, f32[4,2304]{1,0:T(4,128)}, /*index=5*/f32[24,128]{1,0:T(8,128)}, f32[4,768]{1,0:T(4,128)}) custom-call(s32[1280,1]{1,0:T(8,128)} %copy.36.place_col, bf16[1280,768]{1,0:T(8,128)(2,1)} %get-tuple-element.98.d_query, ...), custom_call_target="tpu_custom_call" | custom-call | tf_op jit(solution)/shard_map/pair_tail/pallas_call | solution.py:1744
  356.8 1.9 copy.37
  358.7 3.1 copy.48
  361.9 1.9 copy.49
  363.8 0.6 copy.50
  364.4 0.6 copy.51
  365.0 0.6 copy.52
  365.6 0.6 copy.53
  366.2 0.6 copy.54
  366.8 0.7 copy.55
  367.5 0.7 copy.56
  368.2 0.6 copy.57
  (19 shorter events, 0.0 us)
Async XLA Ops:
  140.0 89.3 %copy-start.10 = (bf16[2,768]{1,0:T(2,128)(2,1)S(1)}, bf16[2,768]{1,0:T(2,128)(2,1)}, u32[]{:S(2)}) copy-start(bf16[2,768]{1,0:T(2,128)(2,1)} %param.40) | copy-start | bytes 9220
  256.4 46.8 %copy-start.6 = (s32[1,1280]{1,0:T(1,128)S(1)}, s32[1,1280]{1,0:T(1,128)}, u32[]{:S(2)}) copy-start(s32[1,1280]{1,0:T(1,128)} %place_row.1) | copy-start | bytes 15364
  358.7 3.1 copy-start
  361.8 2.0 copy-start.9
  361.8 2.6 copy-start.5
  361.8 3.2 copy-start.8
  361.8 3.8 %copy-start.7 = (f32[4,768]{1,0:T(4,128)S(1)}, f32[4,768]{1,0:T(4,128)}, u32[]{:S(2)}) copy-start(f32[4,768]{1,0:T(4,128)} %get-tuple-element.162) | copy-start | bytes 36868
  361.8 4.4 %copy-start.4 = (f32[96,128]{1,0:T(8,128)S(1)}, f32[96,128]{1,0:T(8,128)}, u32[]{:S(2)}) copy-start(f32[96,128]{1,0:T(8,128)} %get-tuple-element.119) | copy-start | bytes 147460
  361.8 5.0 %copy-start.1 = (f32[16,4096]{1,0:T(8,128)S(1)}, f32[16,4096]{1,0:T(8,128)}, u32[]{:S(2)}) copy-start(f32[16,4096]{1,0:T(8,128)} %get-tuple-element.120) | copy-start | bytes 786436
  361.8 5.7 %copy-start.2 = (f32[256,128]{1,0:T(8,128)S(1)}, f32[256,128]{1,0:T(8,128)}, u32[]{:S(2)}) copy-start(f32[256,128]{1,0:T(8,128)} %get-tuple-element.121) | copy-start | bytes 393220
  361.8 6.4 %copy-start.3 = (f32[16,768]{1,0:T(8,128)S(1)}, f32[16,768]{1,0:T(8,128)}, u32[]{:S(2)}) copy-start(f32[16,768]{1,0:T(8,128)} %get-tuple-element.122) | copy-start | bytes 147460
where the time goes:
time: 374 us; the launch traced here: 369 us
  Pallas kernels  351 us (94%)
  local copies, waits for them, and re-layouts  15.6 us (4%)
    pallas_call x1, Pallas kernels, shards(): pl.pallas_call(functools.partial(pair_front_body, kinds, a_rows, b_rows),...  137 us
    pallas_call x1, Pallas kernels, shards(): pl.pallas_call(pair_ffn_body, in_specs=[hbm] * 5, out_specs=[hbm] + [vmem...  88.7 us
    pallas_call x1, Pallas kernels, shards(): pl.pallas_call(pair_tail_body, in_specs=[vmem] * 13 + [hbm] * 4, out_spec...  52.5 us
    pallas_call x1, Pallas kernels, shards(): pl.pallas_call(pair_attention_bwd_body, grid=(pairs,), in_specs=[col_spec...  46.8 us
    pallas_call x1, Pallas kernels, shards(): call(functools.partial(combine_body, expert_count, kinds), (tok // ROW_BL...  26.6 us
    unnamed x33, local copies, waits for them, and re-layouts  12 us

commit v1 on v0

--- a/solution.py
+++ b/solution.py
@@ -233,7 +233,7 @@
 
 def pair_front_body(
     kinds, a_rows, b_rows,
-    lengths, adapters, place_row, hidden, upstream, carry, choices, gain_one, gain_two,
+    lengths, adapters, place_row, hidden, upstream, carry, choices, gains,
     router_in, const_in, in_qkv, in_out, in_a_qkv, in_a_out, in_b_qkv, in_b_out,
     in_gu, in_b_gu, in_dn, in_b_dn, in_a_gu, in_a_dn, *rest,
 ):
@@ -250,6 +250,7 @@
         g_qkv, g_out, own_wide, own_mid, own_thin, sent, slot_rows,
         a_send, a_recv, z_send, e_send, e_recv, out_sems, own_sems, row_send, row_recv,
     ) = rest
+    gain_one, gain_two = gains[0:1, :], gains[1:2, :]
     dp, z = lax.axis_index("dp"), lax.axis_index("expert")
     core, x_bit, y_bit = dp % 2, dp // 2 % 2, dp // 4
     across = dp + 1 - 2 * core
@@ -719,6 +720,10 @@
 
     last_local = pltpu.make_async_copy(sent.at[0], last_sent, row_send.at[3])
     own_local = pltpu.make_async_copy(sent.at[0], came.at[0], row_send.at[0])
+    some = pl.ds(0, last_sent.shape[0] // 2)
+    last_half = remote(
+        last_sent.at[some], came.at[3, some], row_send.at[4], row_recv.at[3], (across, next_z)
+    )
     def fill(n, carry):
         k = (n + 1) % 4
         eid = (z + k) % 2 + 2 * ((core + k // 2) % 2)
@@ -736,6 +741,7 @@
         def _():
             last_local.start()
             last_local.wait()
+            last_half.start()
 
         return carry
 
@@ -747,6 +753,8 @@
     for k in (1, 2):
         rows_out(k).wait_recv()
         rows_out(k).wait_send()
+    last_half.wait_recv()
+    last_half.wait_send()
     own_local.wait()
 
     def attn_sent(n, carry):
@@ -768,9 +776,11 @@
 
 
 def pair_attention_bwd_body(
-    query, key, value, dout, attended, lse, starts, cosine, sine, ga_gu, gb_gu, ga_dn, gb_dn,
-    d_query, d_key, d_value, own_ga_gu, own_gb_gu, own_ga_dn, own_gb_dn,
-    kacc, vacc, r_ga_gu, r_gb_gu, r_ga_dn, r_gb_dn, send_sems, recv_sems,
+    query, key, value, dout, attended, lse, starts, cosine, sine, ga_out, gb_out,
+    ga_gu, gb_gu, ga_dn, gb_dn,
+    d_query, d_key, d_value, own_ga_gu, own_gb_gu, own_ga_dn, own_gb_dn, plane_ga_out, plane_gb_out,
+    kacc, vacc, r_ga_gu, r_gb_gu, r_ga_dn, r_gb_dn, s_ga_out, s_gb_out, r_ga_out, r_gb_out,
+    send_sems, recv_sems, near_send, near_recv,
 ):
     dp, z = lax.axis_index("dp"), lax.axis_index("expert")
     core, spot, half = dp % 2, dp // 2, z // 2
@@ -784,6 +794,20 @@
         (ga_dn, r_ga_dn, own_ga_dn), (gb_dn, r_gb_dn, own_gb_dn),
     )
     owners = 8
+    plane_groups = (
+        (s_ga_out, r_ga_out, plane_ga_out), (s_gb_out, r_gb_out, plane_gb_out),
+    )
+
+    def share(i, d):
+        count = plane_groups[i][1].shape[1]
+        return plane_groups[i][0].at[pl.ds(pl.multiple_of(d * count, 16), count)]
+
+    def near(i, n):
+        goal = (dp + n + 1) % owners
+        return pltpu.make_async_remote_copy(
+            src_ref=share(i, goal), dst_ref=plane_groups[i][1].at[n], send_sem=near_send.at[i, n],
+            recv_sem=near_recv.at[i, n], device_id=(goal, z), device_id_type=MESH_ID,
+        )
 
     def piece(i, d):
         source, target, _ = groups[i]
@@ -809,12 +833,18 @@
 
     @pl.when(pl.program_id(0) == 0)
     def _():
-        senders = []
-        for m in range(owners // 2):
-            device = 2 * m + half
-            senders.append(((device, z), device != dp))
-            senders.append(((device, far), None))
-        start_kernel(None, senders, owners - 1 + away)
+        s_ga_out[...] = ga_out[...].astype(BF16)
+        s_gb_out[...] = gb_out[...].astype(BF16)
+        senders = [((2 * m + half, far), None) for m in range(owners // 2)]
+        senders += [(((dp + n) % owners, z), None) for n in range(1, owners)]
+        start_kernel(None, senders, owners - 1 + owners * away)
+
+        def send_near(n, carry):
+            for i in range(2):
+                near(i, n).start()
+            return carry
+
+        lax.fori_loop(0, owners - 1, send_near, 0)
 
         def send(d, carry):
             mine = at_home & (d == dp)
@@ -867,23 +897,39 @@
                 total = total + target[s].astype(F32)
             out[...] = total
 
+        def finish_near(n, carry):
+            for i in range(2):
+                near(i, n).wait_recv()
+                near(i, n).wait_send()
+            return carry
+
+        lax.fori_loop(0, owners - 1, finish_near, 0)
+        for i, (_, target, out) in enumerate(plane_groups):
+            total = share(i, dp)[...].astype(F32)
+            for n in range(owners - 1):
+                total = total + target[n].astype(F32)
+            out[...] = total
+
 
 def pair_tail_body(
-    place_col, d_query, d_key, d_value, low_qkv, act_one, mask, a_in, b_out, gain, ga_out, gb_out,
-    d_logits, hid_hbm, resid_hbm, w_hbm, out_hbm,
+    place_row, mask, a_in, b_out, gain, a_o, b_o, d_logits,
+    q_hbm, k_hbm, v_hbm, low_hbm, act_hbm, hid_hbm, resid_hbm, w_hbm, out_hbm,
     out, grad_hidden, grad_gate, own_ga_qkv, own_gb_qkv, own_ga_out, own_gb_out,
-    hid_s, d_resid, w_qkv, out_s, high, lower, d_low_all, ga_sum, gb_sum,
-    s_ga_qkv, s_gb_qkv, s_ga_out, s_gb_out, r_ga_qkv, r_gb_qkv, r_ga_out, r_gb_out,
+    d_query, d_key, d_value, low_qkv, act_one,
+    hid_s, d_resid, w_qkv, out_s, place_col, high, lower, d_low_all, ga_sum, gb_sum,
+    s_ga_qkv, s_gb_qkv, r_ga_qkv, r_gb_qkv,
     thin_out, wide_out, thin_in, wide_in, load_sems, send_sems, recv_sems, far_send, far_recv,
 ):
     dp, z = lax.axis_index("dp"), lax.axis_index("expert")
     others, planes = 7, 3
-    tok = place_col.shape[0]
+    tok = place_row.shape[1]
     blocks = tok // ROW_BLOCK
     loads = [
         pltpu.make_async_copy(source, target, load_sems.at[i])
         for i, (source, target) in enumerate(
-            ((w_hbm, w_qkv), (hid_hbm, hid_s), (resid_hbm, d_resid), (out_hbm, out_s))
+            ((q_hbm, d_query), (k_hbm, d_key), (v_hbm, d_value), (low_hbm, low_qkv),
+             (act_hbm, act_one), (w_hbm, w_qkv), (hid_hbm, hid_s), (resid_hbm, d_resid),
+             (out_hbm, out_s))
         )
     ]
     for load in loads:
@@ -914,14 +960,12 @@
         ga_sum[...] += dot_tn(act_one[rows, :], d_low)
         return carry
 
+    for load in loads[:5]:
+        load.wait()
     lax.fori_loop(0, blocks, sums, 0)
     s_ga_qkv[...] = ga_sum[...].astype(BF16)
     s_gb_qkv[...] = gb_sum[...].astype(BF16)
-    s_ga_out[...] = ga_out[...].astype(BF16)
-    s_gb_out[...] = gb_out[...].astype(BF16)
-    groups = (
-        (s_ga_qkv, r_ga_qkv), (s_gb_qkv, r_gb_qkv), (s_ga_out, r_ga_out), (s_gb_out, r_gb_out),
-    )
+    groups = ((s_ga_qkv, r_ga_qkv), (s_gb_qkv, r_gb_qkv))
 
     def share(i, d):
         count = groups[i][1].shape[1]
@@ -935,13 +979,13 @@
         )
 
     def send_near(n, carry):
-        for i in range(4):
+        for i in range(2):
             near(i, n).start()
         return carry
 
     lax.fori_loop(0, others, send_near, 0)
 
-    for load in loads[:3]:
+    for load in loads[5:8]:
         load.wait()
 
     def back(b, carry):
@@ -962,28 +1006,29 @@
         return carry
 
     lax.fori_loop(0, blocks, back, 0)
+    place_col[...] = jnp.broadcast_to(place_row[...].astype(F32), (LANES, tok)).T
 
     def near_done(n, carry):
-        for i in range(4):
+        for i in range(2):
             near(i, n).wait_recv()
         return carry
 
     lax.fori_loop(0, others, near_done, 0)
     totals = []
-    for i in range(4):
+    for i in range(2):
         total = share(i, dp)[...].astype(F32)
         for n in range(others):
             total = total + groups[i][1][n].astype(F32)
         totals.append(total)
-    a_qkv, b_qkv, a_o, b_o = totals
+    a_qkv, b_qkv = totals
     a_count, b_count = a_qkv.shape[0] // 4, b_qkv.shape[0] // 4
     for p in range(4):
         a_rows, b_rows = slice(p * a_count, (p + 1) * a_count), slice(p * b_count, (p + 1) * b_count)
         thin_out[p, :a_count, :LANES] = a_qkv[a_rows].astype(BF16)
-        thin_out[p, :a_count, LANES:] = a_o[a_rows].astype(BF16)
+        thin_out[p, :a_count, LANES:] = a_o[a_rows, :].astype(BF16)
         thin_out[p, a_count:, :] = jnp.zeros((thin_out.shape[1] - a_count, 2 * LANES), BF16)
         wide_out[p] = jnp.concatenate(
-            [b_qkv[b_rows, cols] for cols in parts] + [b_o[b_rows]], axis=0
+            [b_qkv[b_rows, cols] for cols in parts] + [b_o[b_rows, :]], axis=0
         ).astype(BF16)
 
     def far(i, j):
@@ -997,14 +1042,14 @@
     for j in range(planes):
         for i in range(2):
             far(i, j).start()
-    loads[3].wait()
+    loads[8].wait()
 
     top, mid, last = (jnp.where(iota((tok, LANES), 1) < 16, v.astype(F32), 0.0) for v in split_three(d_logits[...]))
     logit_parts = (top + pltpu.roll(mid, 16, 1) + pltpu.roll(last, 32, 1)).astype(BF16)
 
     def to_rows(b, carry):
         rows = block_rows(b)
-        perm = hot_matrix(place_col[rows, :] == iota((ROW_BLOCK, tok), 1))
+        perm = hot_matrix(place_col[rows, 0:1].astype(jnp.int32) == iota((ROW_BLOCK, tok), 1))
         out[rows, :] = dot(perm, out_s[...]).astype(BF16)
         grad_hidden[rows, :] = dot(perm, high[...]) + dot(perm, lower[...])
         moved = dot(perm, logit_parts)
@@ -1029,7 +1074,7 @@
     own_gb_out[...] = wide[3 * b_count : 4 * b_count]
 
     def sent(n, carry):
-        for i in range(4):
+        for i in range(2):
             near(i, n).wait_send()
         return carry
 
@@ -1037,6 +1082,12 @@
     for j in range(planes):
         for i in range(2):
             far(i, j).wait_send()
+
+
+def settle_body(*refs):
+    count = len(refs) // 2
+    for n, (source, target) in enumerate(zip(refs[:count], refs[count:])):
+        target[...] = source[...].T[: target.shape[0]] if n == 0 else source[...]
 
 
 def split_three(values):
@@ -1175,11 +1226,12 @@
     start_kernel(None, [(peer(k), None) for k in (1, 2, 3)], 3)
 
     half = last_sent.shape[0] // 2
-    late = pl.ds(0, 2 * half)
+    early, late = pl.ds(0, half), pl.ds(half, half)
 
     def had_in(k):
         return pltpu.make_async_copy(had.at[k], came.at[k], came_sems.at[k])
 
+    early_in = pltpu.make_async_copy(had.at[3, early], came.at[3, early], came_sems.at[3])
     last_out = pltpu.make_async_remote_copy(
         src_ref=last_sent.at[late], dst_ref=came.at[3, late], send_sem=last_sems.at[0],
         recv_sem=last_sems.at[1], device_id=peer(3), device_id_type=MESH_ID,
@@ -1194,6 +1246,7 @@
     last_out.start()
     for k in (1, 0, 2):
         had_in(k).start()
+    early_in.start()
 
     gu_rows = w_gu.shape[0] // wide.shape[0]
     up_rows = b_gu.shape[0] // wide.shape[0]
@@ -1219,7 +1272,7 @@
         pltpu.make_async_copy(target, target, load_sems.at[i]).wait()
 
     def source_step(s, carry):
-        k = s + 1 - 2 * (s % 2)
+        k = jnp.where(s < 2, 1 + 2 * s, 2 * s - 4)
 
         @pl.when(k != 3)
         def _():
@@ -1227,6 +1280,7 @@
 
         @pl.when(k == 3)
         def _():
+            early_in.wait()
             last_out.wait_recv()
 
         back[k, :, :MODEL_WIDTH], back[k, :, MODEL_WIDTH:] = ffn_math(
@@ -1485,7 +1539,8 @@
     gu_rows, up_rows, dn_rows = (
         gate_upward_weight.shape[1], adapter_out_gate.shape[1], down_weight.shape[1],
     )
-    gain_one, gain_two = attention_gain[None, :], feedfwd_gain[None, :]
+    gains = jnp.stack([attention_gain, feedfwd_gain])
+    gain_one, gain_two = gains[0:1], gains[1:2]
     const_value = constant_value.astype(F32)
     sent_width = 2 * width + LANES
     full = whole
@@ -1521,7 +1576,7 @@
             wide, mid, thin, came, last_sent,
         ) = pl.pallas_call(
             functools.partial(pair_front_body, kinds, a_rows, b_rows),
-            in_specs=[smem] * 2 + [vmem] * 15 + [hbm] * 6,
+            in_specs=[smem] * 2 + [vmem] * 14 + [hbm] * 6,
             out_specs=[hbm] * (FRONT_KEPT + 5),
             out_shape=shapes
             + [sds((dp_size,) + shape, BF16) for shape in packed]
@@ -1544,7 +1599,7 @@
             ),
             name="pair_front",
         )(sequence_length, sequence_adapter, token_stream_place, hidden_input, output_gradient,
-          gate_carryover.T, expert_choice_index.T, gain_one, gain_two, router_weight.T,
+          gate_carryover.T, expert_choice_index.T, gains, router_weight.T,
           constant_gate.T,
           query_key_weight, output_weight, adapter_in_query, adapter_in_output, adapter_out_query,
           adapter_out_output, gate_upward_weight, adapter_out_gate, down_weight, adapter_out_down,
@@ -1723,36 +1778,47 @@
             sds((gu_rows, LANES), F32), sds((up_rows, 2 * FEEDFWD_WIDTH), F32),
             sds((dn_rows, LANES), F32), sds((up_rows, width), F32),
         ]
-        d_query, d_key, d_value, *expert_owned = pl.pallas_call(
+        plane_shapes = [
+            sds((width // dp_size, LANES), F32), sds((LANES // dp_size, width), F32),
+        ]
+        d_query, d_key, d_value, *expert_owned, plane_ga, plane_gb = pl.pallas_call(
             pair_attention_bwd_body,
             grid=(pairs,),
             in_specs=[col_spec(tok)] * 5
-            + [full((lse_rows, tok)), full((1, tok)), full((tok, LANES)), full((tok, LANES))]
+            + [full((lse_rows, tok)), full((1, tok)), full((tok, LANES)), full((tok, LANES)),
+               full((width, LANES)), full((LANES, width))]
             + [hbm] * 4,
-            out_specs=[col_spec(tok)] * 3 + [full(s.shape) for s in own_shapes],
-            out_shape=[sds((tok, width), BF16)] * 3 + own_shapes,
+            out_specs=[col_spec(tok)] * 3 + [full(s.shape) for s in own_shapes + plane_shapes],
+            out_shape=[sds((tok, width), BF16)] * 3 + own_shapes + plane_shapes,
             scratch_shapes=[pltpu.VMEM((tok, LANES), F32), pltpu.VMEM((tok, LANES), F32)]
             + [pltpu.VMEM((dp_size,) + s.shape, BF16) for s in own_shapes]
-            + [pltpu.SemaphoreType.DMA((4, dp_size)), pltpu.SemaphoreType.DMA((4, dp_size))],
+            + [pltpu.VMEM((width, LANES), BF16), pltpu.VMEM((LANES, width), BF16)]
+            + [pltpu.VMEM((dp_size - 1,) + s.shape, BF16) for s in plane_shapes]
+            + [pltpu.SemaphoreType.DMA((4, dp_size)), pltpu.SemaphoreType.DMA((4, dp_size)),
+               pltpu.SemaphoreType.DMA((2, dp_size)), pltpu.SemaphoreType.DMA((2, dp_size))],
             compiler_params=pltpu.CompilerParams(collective_id=2, **flow),
             name="pair_attention_bwd",
-        )(query, key, value, d_attended, attn_low, lse, starts, cosine, sine,
+        )(query, key, value, d_attended, attn_low, lse, starts, cosine, sine, ga_out, gb_out,
           ga_gu, gb_gu, ga_dn, gb_dn)
-        sum_shapes = [(width, LANES), (LANES, 3 * width), (width, LANES), (LANES, width)]
+        sum_shapes = [(width, LANES), (LANES, 3 * width)]
         got_shapes = [(dp_size - 1, a // dp_size, b) for a, b in sum_shapes]
         thin_rows = -(-a_rows // 16) * 16
-        output, grad_hidden, grad_gate, *attn_owned = pl.pallas_call(
+        tail_shapes = [
+            sds((tok, width), BF16), sds((tok, width), F32), sds((tok, LANES), F32),
+            sds((a_rows, LANES), F32), sds((b_rows, 3 * width), F32),
+            sds((a_rows, LANES), F32), sds((b_rows, width), F32),
+        ]
+        tail = pl.pallas_call(
             pair_tail_body,
-            in_specs=[vmem] * 13 + [hbm] * 4,
+            in_specs=[vmem] * 8 + [hbm] * 9,
             out_specs=[vmem] * 7,
-            out_shape=[
-                sds((tok, width), BF16), sds((tok, width), F32), sds((tok, LANES), F32),
-                sds((a_rows, LANES), F32), sds((b_rows, 3 * width), F32),
-                sds((a_rows, LANES), F32), sds((b_rows, width), F32),
-            ],
+            out_shape=tail_shapes,
             scratch_shapes=[
+                *[pltpu.VMEM((tok, width), BF16) for _ in range(3)],
+                pltpu.VMEM((tok, LANES), BF16), pltpu.VMEM((tok, width), BF16),
                 pltpu.VMEM((tok, width), BF16), pltpu.VMEM((tok, width), F32),
                 pltpu.VMEM((width, 3 * width), BF16), pltpu.VMEM((tok, width), BF16),
+                pltpu.VMEM((tok, LANES), F32),
                 pltpu.VMEM((tok, width), BF16), pltpu.VMEM((tok, width), BF16),
                 pltpu.VMEM((tok, LANES), BF16),
                 pltpu.VMEM((width, LANES), F32), pltpu.VMEM((LANES, 3 * width), F32),
@@ -1761,15 +1827,30 @@
                 pltpu.VMEM((expert_count, 4 * b_rows, width), BF16),
                 pltpu.VMEM((expert_count - 1, thin_rows, 2 * LANES), BF16),
                 pltpu.VMEM((expert_count - 1, 4 * b_rows, width), BF16),
-                pltpu.SemaphoreType.DMA((4,)),
-                pltpu.SemaphoreType.DMA((4, dp_size - 1)), pltpu.SemaphoreType.DMA((4, dp_size - 1)),
+                pltpu.SemaphoreType.DMA((9,)),
+                pltpu.SemaphoreType.DMA((2, dp_size - 1)), pltpu.SemaphoreType.DMA((2, dp_size - 1)),
                 pltpu.SemaphoreType.DMA((2, expert_count - 1)),
                 pltpu.SemaphoreType.DMA((2, expert_count - 1)),
             ],
             compiler_params=pltpu.CompilerParams(collective_id=3, **flow),
             name="pair_tail",
-        )(place[:, None], d_query, d_key, d_value, low_qkv, act_one, mask, a_qkv, b_qkv, gain_one,
-          ga_out, gb_out, d_logits, hid_s, d_resid, w_qkv, out_s)
+        )(token_stream_place, mask, a_qkv, b_qkv, gain_one, plane_ga, plane_gb, d_logits,
+          d_query, d_key, d_value, low_qkv, act_one, hid_s, d_resid, w_qkv, out_s)
+        output, grad_hidden, grad_gate, *attn_owned = tail
+        small_owned = [*attn_owned, *expert_owned]
+        small_specs = [full(v.shape) for v in small_owned]
+        grad_gate, output, grad_hidden, *owned = call(
+            settle_body,
+            (blocks,),
+            [row_spec(LANES), row_spec(width), row_spec(width)] + small_specs,
+            [pl.BlockSpec((kinds, ROW_BLOCK), lambda i: (0, i)), row_spec(width), row_spec(width)]
+            + small_specs,
+            [sds((kinds, tok), F32), sds((tok, width), BF16), sds((tok, width), F32)]
+            + [sds(v.shape, F32) for v in small_owned],
+            name="settle",
+        )(grad_gate, output, grad_hidden, *small_owned)
+        attn_owned, expert_owned = owned[:4], owned[4:]
+        grad_gate = grad_gate.T
         return (
             output, grad_hidden, grad_gate[:, :kinds], *attn_owned,
             *[expert_owned[i][None] for i in range(4)],

time: 374 us -> 360 us (0.963)
  local copies, waits for them, and re-layouts: 15.6 us -> 1.39 us
    unnamed x33 -> x6, local copies, waits for them, and re-layouts: 12 us -> 0.01 us
    pallas_call x1, Pallas kernels: 88.7 us -> 79.3 us  [shards(): pl.pallas_call(pair_ffn_body, in_specs=[hbm] * 5, out_specs=[hbm] + [vmem...]
    pallas_call x1, Pallas kernels: 137 us -> 141 us  [shards(): pl.pallas_call(functools.partial(pair_front_body, kinds, a_rows, b_rows),...]
    pallas_call x1 -> x2, Pallas kernels: 52.5 us -> 52.4 us  [the longest x1 45.1 us: shards(): pl.pallas_call(pair_tail_body, in_specs=[vmem] * 8 + [hbm] * 9, out_specs...]
where the time goes in v1:
time: 360 us; the launch traced here: 354 us
  Pallas kernels  350 us (97%)
    pallas_call x1, Pallas kernels, shards(): pl.pallas_call(functools.partial(pair_front_body, kinds, a_rows, b_rows),...  141 us
    pallas_call x1, Pallas kernels, shards(): pl.pallas_call(pair_ffn_body, in_specs=[hbm] * 5, out_specs=[hbm] + [vmem...  79.3 us
    pallas_call x1, Pallas kernels, shards(): pl.pallas_call(pair_attention_bwd_body, grid=(pairs,), in_specs=[col_spec...  50.4 us
    pallas_call x1, Pallas kernels, shards(): pl.pallas_call(pair_tail_body, in_specs=[vmem] * 8 + [hbm] * 9, out_specs...  45.1 us
    pallas_call x1, Pallas kernels, shards(): call(functools.partial(combine_body, expert_count, kinds), (tok // ROW_BL...  26.6 us
    pallas_call x1, Pallas kernels, shards(): call(settle_body, (blocks,), [row_spec(LANES), row_spec(width), row_spec(...  7.33 us

profile of v1, /device:TPU:1, one launch (start us, length us, event | category | flops | bytes accessed | tf_op | source)
XLA Modules:
  0.0 353.9 jit_solution(3647576114630359813)
XLA Ops:
  0.6 0.7 stack.10.gain
  1.3 0.0 copy-start.1
  1.3 0.7 stack.9.gain
  2.0 0.0 copy-start
  2.0 0.6 pad_maximum_fusion.gains
  2.6 141.1 %pair_front.1 = (bf16[1280,768]{1,0:T(8,128)(2,1)}, bf16[1280,768]{1,0:T(8,128)(2,1)}, f32[1280,128]{1,0:T(8,128)}, bf16[1280,768]{1,0:T(8,128)(2,1)}, bf16[1280...) custom-call(s32[1,5]{1,0:T(1,128)} %lengths.1, ...), custom_call_target="tpu_custom_call" | custom-call | tf_op jit(solution)/shard_map/pair_front/pallas_call | solution.py:1577
  143.7 0.0 copy-done.1
  143.7 0.0 copy-done
  143.8 0.0 copy-start.2
  143.8 79.3 %pair_ffn.1 = (bf16[4,416,1536]{2,1,0:T(8,128)(2,1)}, bf16[768,128]{1,0:T(8,128)(2,1)}, bf16[128,4096]{1,0:T(8,128)(2,1)}, bf16[2048,128]{1,0:T(8,128)(2,1)}, bf16[128,768]{1,0:T(8,128)(2,1)}) custom-call(bf16[4,416,1664]{2,1,0:T(8,128)(2,1)} %get-tuple-element.94.had, bf16[416,1664]{1,0:T(8,128)(2,1)} %get-tuple-element.95.last_sent, ...), custom_call_target="tpu_custom_call" | custom-call | tf_op jit(solution)/shard_map/pair_ffn/pallas_call | solution.py:1715
  223.1 0.5 iota_xor_fusion.eids
  223.6 0.0 copy-done.2
  223.6 0.6 convert_element_type.3.const_value
  224.2 26.6 %combine.1 = (bf16[1280,768]{1,0:T(8,128)(2,1)}, f32[1280,768]{1,0:T(8,128)}, bf16[1280,768]{1,0:T(8,128)(2,1)}, f32[1280,128]{1,0:T(8,128)}, f32[768,128]{1,0:T(8,128)}, /*index=5*/f32[128,768]{1,0:T(8,128)}) custom-call(s32[4]{0:T(128)} %iota_xor_fusion.eids, f32[1280,768]{1,0:T(8,128)} %get-tuple-element.86.resid, ...), custom_call_target="tpu_custom_call" | custom-call | tf_op jit(solution)/shard_map/combine/pallas_call | solution.py:1760
  250.8 50.4 %pair_attention_bwd.1 = (bf16[1280,768]{1,0:T(8,128)(2,1)}, bf16[1280,768]{1,0:T(8,128)(2,1)}, bf16[1280,768]{1,0:T(8,128)(2,1)}, f32[96,128]{1,0:T(8,128)}, f32...) custom-call(bf16[1280,768]{1,0:T(8,128)(2,1)} %get-tuple-element.83.quer, ...), custom_call_target="tpu_custom_call" | custom-call | tf_op jit(solution)/shard_map/pair_attention_bwd/pallas_call | solution.py:1784
  301.2 45.1 %pair_tail.1 = (bf16[1280,768]{1,0:T(8,128)(2,1)}, f32[1280,768]{1,0:T(8,128)}, f32[1280,128]{1,0:T(8,128)}, f32[24,128]{1,0:T(8,128)}, f32[4,2304]{1,0:T(4,128)}, /*index=5*/f32[24,128]{1,0:T(8,128)}, f32[4,768]{1,0:T(4,128)}) custom-call(s32[1,1280]{1,0:T(1,128)} %place_row.3, bf16[1280,128]{1,0:T(8,128)(2,1)} %get-tuple-element.80.mask, ...), custom_call_target="tpu_custom_call" | custom-call | tf_op jit(solution)/shard_map/pair_tail/pallas_call | solution.py:1811
  346.2 7.3 %settle.1 = (f32[8,1280]{1,0:T(8,128)}, bf16[1280,768]{1,0:T(8,128)(2,1)}, f32[1280,768]{1,0:T(8,128)}, f32[24,128]{1,0:T(8,128)}, f32[4,2304]{1,0:T(4,128)}, /*...) custom-call(f32[1280,128]{1,0:T(8,128)} %get-tuple-element.127.refs_, ...), custom_call_target="tpu_custom_call" | custom-call | tf_op jit(solution)/shard_map/settle/pallas_call | solution.py:1842
Async XLA Ops:
  1.3 142.4 %copy-start.1 = (bf16[1,768]{1,0:T(2,128)(2,1)}, bf16[1,768]{1,0:T(2,128)(2,1)S(1)}, u32[]{:S(2)}) copy-start(bf16[1,768]{1,0:T(2,128)(2,1)S(1)} %stack.10.gain) | copy-start | bytes 4612
  2.0 141.7 %copy-start = (bf16[1,768]{1,0:T(2,128)(2,1)}, bf16[1,768]{1,0:T(2,128)(2,1)S(1)}, u32[]{:S(2)}) copy-start(bf16[1,768]{1,0:T(2,128)(2,1)S(1)} %stack.9.gain) | copy-start | bytes 4612
  143.8 79.8 %copy-start.2 = (bf16[2,768]{1,0:T(2,128)(2,1)S(1)}, bf16[2,768]{1,0:T(2,128)(2,1)}, u32[]{:S(2)}) copy-start(bf16[2,768]{1,0:T(2,128)(2,1)} %param.40) | copy-start | bytes 9220

commit v2 on v1

--- a/solution.py
+++ b/solution.py
@@ -779,65 +779,85 @@
     query, key, value, dout, attended, lse, starts, cosine, sine, ga_out, gb_out,
     ga_gu, gb_gu, ga_dn, gb_dn,
     d_query, d_key, d_value, own_ga_gu, own_gb_gu, own_ga_dn, own_gb_dn, plane_ga_out, plane_gb_out,
-    kacc, vacc, r_ga_gu, r_gb_gu, r_ga_dn, r_gb_dn, s_ga_out, s_gb_out, r_ga_out, r_gb_out,
-    send_sems, recv_sems, near_send, near_recv,
+    kacc, vacc, *rest,
 ):
+    mine, got, halves, final = (rest[4 * n : 4 * n + 4] for n in range(4))
+    (
+        s_ga_out, s_gb_out, r_ga_out, r_gb_out,
+        own_sems, side_send, side_recv, end_send, end_recv, near_send, near_recv,
+    ) = rest[16:]
     dp, z = lax.axis_index("dp"), lax.axis_index("expert")
     core, spot, half = dp % 2, dp // 2, z // 2
-    own = z % 2 + 2 * core
     far = (z + 2) % 4
-    at_home = core == half
-    away = 1 - (core * half + (1 - core) * (1 - half))
-    slot = 2 * spot + away
-    groups = (
-        (ga_gu, r_ga_gu, own_ga_gu), (gb_gu, r_gb_gu, own_gb_gu),
-        (ga_dn, r_ga_dn, own_ga_dn), (gb_dn, r_gb_dn, own_gb_dn),
-    )
-    owners = 8
+    across = dp + 1 - 2 * core
+    home = core == half
+    away = core + half - 2 * core * half
+    owners, spots = 8, 4
+    sources = (ga_gu, gb_gu, ga_dn, gb_dn)
+    outs = (own_ga_gu, own_gb_gu, own_ga_dn, own_gb_dn)
     plane_groups = (
         (s_ga_out, r_ga_out, plane_ga_out), (s_gb_out, r_gb_out, plane_gb_out),
     )
 
+    def remote(source, target, send, recv, device):
+        return pltpu.make_async_remote_copy(
+            src_ref=source, dst_ref=target, send_sem=send, recv_sem=recv,
+            device_id=device, device_id_type=MESH_ID,
+        )
+
     def share(i, d):
         count = plane_groups[i][1].shape[1]
         return plane_groups[i][0].at[pl.ds(pl.multiple_of(d * count, 16), count)]
 
     def near(i, n):
         goal = (dp + n + 1) % owners
-        return pltpu.make_async_remote_copy(
-            src_ref=share(i, goal), dst_ref=plane_groups[i][1].at[n], send_sem=near_send.at[i, n],
-            recv_sem=near_recv.at[i, n], device_id=(goal, z), device_id_type=MESH_ID,
-        )
-
-    def piece(i, d):
-        source, target, _ = groups[i]
-        count = target.shape[1]
-        return source.at[pl.ds(pl.multiple_of(d * count, 16), count)]
-
-    def push(i, d):
-        return pltpu.make_async_remote_copy(
-            src_ref=piece(i, d), dst_ref=groups[i][1].at[slot], send_sem=send_sems.at[i, d],
-            recv_sem=recv_sems.at[i, slot], device_id=(d, own), device_id_type=MESH_ID,
-        )
+        return remote(
+            share(i, goal), plane_groups[i][1].at[n], near_send.at[i, n], near_recv.at[i, n], (goal, z)
+        )
+
+    def quarter(i, m):
+        count = mine[i].shape[0]
+        return sources[i].at[pl.ds(pl.multiple_of(m * count, 16), count)]
 
     def keep(i):
-        return pltpu.make_async_copy(
-            piece(i, dp), groups[i][1].at[2 * spot], recv_sems.at[i, 2 * spot]
-        )
-
-    def arrival(i, s):
-        return pltpu.make_async_remote_copy(
-            src_ref=piece(i, 0), dst_ref=groups[i][1].at[s], send_sem=send_sems.at[i, 0],
-            recv_sem=recv_sems.at[i, s], device_id=(0, own), device_id_type=MESH_ID,
-        )
-
-    @pl.when(pl.program_id(0) == 0)
+        return pltpu.make_async_copy(quarter(i, spot), mine[i], own_sems.at[i])
+
+    def side(i, n):
+        goal = (spot + n + 1) % spots
+        return remote(
+            quarter(i, goal), got[i].at[n], side_send.at[i, n], side_recv.at[i, n],
+            (2 * goal + core, z),
+        )
+
+    def to_across(i):
+        return remote(
+            halves[i].at[1 - core], final[i].at[0], end_send.at[i, 0], end_recv.at[i, 0], (across, z)
+        )
+
+    def to_far(i, h):
+        return remote(
+            halves[i].at[h], final[i].at[1], end_send.at[i, h], end_recv.at[i, 1],
+            (dp - core + h, far),
+        )
+
+    step = pl.program_id(0)
+
+    @pl.when(step == 0)
     def _():
         s_ga_out[...] = ga_out[...].astype(BF16)
         s_gb_out[...] = gb_out[...].astype(BF16)
-        senders = [((2 * m + half, far), None) for m in range(owners // 2)]
+        senders = [((dp - core + half, far), None)]
         senders += [(((dp + n) % owners, z), None) for n in range(1, owners)]
-        start_kernel(None, senders, owners - 1 + owners * away)
+        start_kernel(None, senders, owners - 1 + 2 * away)
+        for i in range(4):
+            keep(i).start()
+
+        def send_side(n, carry):
+            for i in range(4):
+                side(i, n).start()
+            return carry
+
+        lax.fori_loop(0, spots - 1, send_side, 0)
 
         def send_near(n, carry):
             for i in range(2):
@@ -846,56 +866,55 @@
 
         lax.fori_loop(0, owners - 1, send_near, 0)
 
-        def send(d, carry):
-            mine = at_home & (d == dp)
-
-            @pl.when(mine)
-            def _():
-                for i in range(4):
-                    keep(i).start()
-
-            @pl.when(jnp.logical_not(mine))
-            def _():
-                for i in range(4):
-                    push(i, d).start()
-
-            return carry
-
-        lax.fori_loop(0, owners, send, 0)
+    @pl.when(step == pl.num_programs(0) - 2)
+    def _():
+        for i in range(4):
+            keep(i).wait()
+            total = mine[i][...].astype(F32)
+            for n in range(spots - 1):
+                side(i, n).wait_recv()
+                total = total + got[i][n].astype(F32)
+            count = halves[i].shape[1]
+            for h in range(2):
+                halves[i][h] = total[h * count : (h + 1) * count].astype(BF16)
+
+            @pl.when(home)
+            def _(i=i):
+                to_across(i).start()
+
+            @pl.when(jnp.logical_not(home))
+            def _(i=i):
+                for h in range(2):
+                    to_far(i, h).start()
 
     attention_bwd_body(
         query, key, value, dout, attended, lse, starts, cosine, sine, d_query, d_key, d_value,
         kacc, vacc,
     )
 
-    @pl.when(pl.program_id(0) == pl.num_programs(0) - 1)
+    @pl.when(step == pl.num_programs(0) - 1)
     def _():
-        def finish(s, carry):
-            mine = at_home & (s == 2 * spot)
-
-            @pl.when(mine)
-            def _():
-                for i in range(4):
-                    keep(i).wait()
-
-            @pl.when(jnp.logical_not(mine))
-            def _():
-                for i in range(4):
-                    arrival(i, s).wait_recv()
-
-            @pl.when(jnp.logical_not(at_home & (s == dp)))
-            def _():
-                for i in range(4):
-                    push(i, s).wait_send()
-
+        for i in range(4):
+            to_far(i, 0).wait_recv()
+
+            @pl.when(home)
+            def _(i=i):
+                outs[i][...] = halves[i][core].astype(F32) + final[i][1].astype(F32)
+                to_across(i).wait_send()
+
+            @pl.when(jnp.logical_not(home))
+            def _(i=i):
+                to_across(i).wait_recv()
+                outs[i][...] = final[i][0].astype(F32) + final[i][1].astype(F32)
+                for h in range(2):
+                    to_far(i, h).wait_send()
+
+        def sent_side(n, carry):
+            for i in range(4):
+                side(i, n).wait_send()
             return carry
 
-        lax.fori_loop(0, owners, finish, 0)
-        for _, target, out in groups:
-            total = target[0].astype(F32)
-            for s in range(1, owners):
-                total = total + target[s].astype(F32)
-            out[...] = total
+        lax.fori_loop(0, spots - 1, sent_side, 0)
 
         def finish_near(n, carry):
             for i in range(2):
@@ -1791,11 +1810,15 @@
             out_specs=[col_spec(tok)] * 3 + [full(s.shape) for s in own_shapes + plane_shapes],
             out_shape=[sds((tok, width), BF16)] * 3 + own_shapes + plane_shapes,
             scratch_shapes=[pltpu.VMEM((tok, LANES), F32), pltpu.VMEM((tok, LANES), F32)]
-            + [pltpu.VMEM((dp_size,) + s.shape, BF16) for s in own_shapes]
+            + [pltpu.VMEM((2 * s.shape[0], s.shape[1]), BF16) for s in own_shapes]
+            + [pltpu.VMEM((3, 2 * s.shape[0], s.shape[1]), BF16) for s in own_shapes]
+            + [pltpu.VMEM((2,) + s.shape, BF16) for s in own_shapes * 2]
             + [pltpu.VMEM((width, LANES), BF16), pltpu.VMEM((LANES, width), BF16)]
             + [pltpu.VMEM((dp_size - 1,) + s.shape, BF16) for s in plane_shapes]
-            + [pltpu.SemaphoreType.DMA((4, dp_size)), pltpu.SemaphoreType.DMA((4, dp_size)),
-               pltpu.SemaphoreType.DMA((2, dp_size)), pltpu.SemaphoreType.DMA((2, dp_size))],
+            + [pltpu.SemaphoreType.DMA((4,)), pltpu.SemaphoreType.DMA((4, 3)),
+               pltpu.SemaphoreType.DMA((4, 3)), pltpu.SemaphoreType.DMA((4, 2)),
+               pltpu.SemaphoreType.DMA((4, 2)), pltpu.SemaphoreType.DMA((2, dp_size)),
+               pltpu.SemaphoreType.DMA((2, dp_size))],
             compiler_params=pltpu.CompilerParams(collective_id=2, **flow),
             name="pair_attention_bwd",
         )(query, key, value, d_attended, attn_low, lse, starts, cosine, sine, ga_out, gb_out,

time: 360 us -> 347 us (0.964)
  Pallas kernels: 350 us -> 338 us
    pallas_call x1, Pallas kernels: 45.1 us -> 34 us  [shards(): pl.pallas_call(pair_tail_body, in_specs=[vmem] * 8 + [hbm] * 9, out_specs...]
where the time goes in v2:
time: 347 us; the launch traced here: 342 us
  Pallas kernels  338 us (97%)
    pallas_call x1, Pallas kernels, shards(): pl.pallas_call(functools.partial(pair_front_body, kinds, a_rows, b_rows),...  141 us
    pallas_call x1, Pallas kernels, shards(): pl.pallas_call(pair_ffn_body, in_specs=[hbm] * 5, out_specs=[hbm] + [vmem...  79.3 us
    pallas_call x1, Pallas kernels, shards(): pl.pallas_call(pair_attention_bwd_body, grid=(pairs,), in_specs=[col_spec...  49.3 us
    pallas_call x1, Pallas kernels, shards(): pl.pallas_call(pair_tail_body, in_specs=[vmem] * 8 + [hbm] * 9, out_specs...  34 us
    pallas_call x1, Pallas kernels, shards(): call(functools.partial(combine_body, expert_count, kinds), (tok // ROW_BL...  26.6 us
    pallas_call x1, Pallas kernels, shards(): call(settle_body, (blocks,), [row_spec(LANES), row_spec(width), row_spec(...  7.33 us

profile of v2, /device:TPU:1, one launch (start us, length us, event | category | flops | bytes accessed | tf_op | source)
XLA Modules:
  0.0 341.7 jit_solution(15117808642014872588)
XLA Ops:
  0.6 0.7 stack.10.gain
  1.3 0.0 copy-start.1
  1.3 0.7 stack.9.gain
  2.0 0.0 copy-start
  2.0 0.6 pad_maximum_fusion.gains
  2.6 141.1 %pair_front.1 = (bf16[1280,768]{1,0:T(8,128)(2,1)}, bf16[1280,768]{1,0:T(8,128)(2,1)}, f32[1280,128]{1,0:T(8,128)}, bf16[1280,768]{1,0:T(8,128)(2,1)}, bf16[1280...) custom-call(s32[1,5]{1,0:T(1,128)} %lengths.1, ...), custom_call_target="tpu_custom_call" | custom-call | tf_op jit(solution)/shard_map/pair_front/pallas_call | solution.py:1596
  143.7 0.0 copy-done.1
  143.7 0.0 copy-done
  143.8 0.0 copy-start.2
  143.8 79.3 %pair_ffn.1 = (bf16[4,416,1536]{2,1,0:T(8,128)(2,1)}, bf16[768,128]{1,0:T(8,128)(2,1)}, bf16[128,4096]{1,0:T(8,128)(2,1)}, bf16[2048,128]{1,0:T(8,128)(2,1)}, bf16[128,768]{1,0:T(8,128)(2,1)}) custom-call(bf16[4,416,1664]{2,1,0:T(8,128)(2,1)} %get-tuple-element.94.had, bf16[416,1664]{1,0:T(8,128)(2,1)} %get-tuple-element.95.last_sent, ...), custom_call_target="tpu_custom_call" | custom-call | tf_op jit(solution)/shard_map/pair_ffn/pallas_call | solution.py:1734
  223.1 0.5 iota_xor_fusion.eids
  223.6 0.0 copy-done.2
  223.6 0.6 convert_element_type.3.const_value
  224.2 26.6 %combine.1 = (bf16[1280,768]{1,0:T(8,128)(2,1)}, f32[1280,768]{1,0:T(8,128)}, bf16[1280,768]{1,0:T(8,128)(2,1)}, f32[1280,128]{1,0:T(8,128)}, f32[768,128]{1,0:T(8,128)}, /*index=5*/f32[128,768]{1,0:T(8,128)}) custom-call(s32[4]{0:T(128)} %iota_xor_fusion.eids, f32[1280,768]{1,0:T(8,128)} %get-tuple-element.86.resid, ...), custom_call_target="tpu_custom_call" | custom-call | tf_op jit(solution)/shard_map/combine/pallas_call | solution.py:1779
  250.8 49.3 %pair_attention_bwd.1 = (bf16[1280,768]{1,0:T(8,128)(2,1)}, bf16[1280,768]{1,0:T(8,128)(2,1)}, bf16[1280,768]{1,0:T(8,128)(2,1)}, f32[96,128]{1,0:T(8,128)}, f32...) custom-call(bf16[1280,768]{1,0:T(8,128)(2,1)} %get-tuple-element.83.quer, ...), custom_call_target="tpu_custom_call" | custom-call | tf_op jit(solution)/shard_map/pair_attention_bwd/pallas_call | solution.py:1803
  300.0 34.0 %pair_tail.1 = (bf16[1280,768]{1,0:T(8,128)(2,1)}, f32[1280,768]{1,0:T(8,128)}, f32[1280,128]{1,0:T(8,128)}, f32[24,128]{1,0:T(8,128)}, f32[4,2304]{1,0:T(4,128)}, /*index=5*/f32[24,128]{1,0:T(8,128)}, f32[4,768]{1,0:T(4,128)}) custom-call(s32[1,1280]{1,0:T(1,128)} %place_row.3, bf16[1280,128]{1,0:T(8,128)(2,1)} %get-tuple-element.80.mask, ...), custom_call_target="tpu_custom_call" | custom-call | tf_op jit(solution)/shard_map/pair_tail/pallas_call | solution.py:1834
  334.1 7.3 %settle.1 = (f32[8,1280]{1,0:T(8,128)}, bf16[1280,768]{1,0:T(8,128)(2,1)}, f32[1280,768]{1,0:T(8,128)}, f32[24,128]{1,0:T(8,128)}, f32[4,2304]{1,0:T(4,128)}, /*...) custom-call(f32[1280,128]{1,0:T(8,128)} %get-tuple-element.127.refs_, ...), custom_call_target="tpu_custom_call" | custom-call | tf_op jit(solution)/shard_map/settle/pallas_call | solution.py:1865
Async XLA Ops:
  1.3 142.4 %copy-start.1 = (bf16[1,768]{1,0:T(2,128)(2,1)}, bf16[1,768]{1,0:T(2,128)(2,1)S(1)}, u32[]{:S(2)}) copy-start(bf16[1,768]{1,0:T(2,128)(2,1)S(1)} %stack.10.gain) | copy-start | bytes 4612
  2.0 141.7 %copy-start = (bf16[1,768]{1,0:T(2,128)(2,1)}, bf16[1,768]{1,0:T(2,128)(2,1)S(1)}, u32[]{:S(2)}) copy-start(bf16[1,768]{1,0:T(2,128)(2,1)S(1)} %stack.9.gain) | copy-start | bytes 4612
  143.8 79.8 %copy-start.2 = (bf16[2,768]{1,0:T(2,128)(2,1)S(1)}, bf16[2,768]{1,0:T(2,128)(2,1)}, u32[]{:S(2)}) copy-start(bf16[2,768]{1,0:T(2,128)(2,1)} %param.40) | copy-start | bytes 9220

commit v3 on v2

--- a/solution.py
+++ b/solution.py
@@ -239,7 +239,7 @@
 ):
     count = FRONT_KEPT
     outs, rest = rest[:count], rest[count:]
-    (all_wide, all_mid, all_thin, came, last_sent), rest = rest[:5], rest[5:]
+    (all_wide, all_mid, all_thin, came, last_sent, came_kinds), rest = rest[:6], rest[6:]
     kept, rest = rest[:count], rest[count:]
     (
         hid_s, dy_s, small_s, act_one, low_qkv, mask, starts, cosine, sine, router,
@@ -247,7 +247,7 @@
         attn_low, lse, low_out, resid, act_two, gate, slot,
     ) = kept
     (
-        g_qkv, g_out, own_wide, own_mid, own_thin, sent, slot_rows,
+        g_qkv, g_out, own_wide, own_mid, own_thin, sent, sent_kinds, slot_rows,
         a_send, a_recv, z_send, e_send, e_recv, out_sems, own_sems, row_send, row_recv,
     ) = rest
     gain_one, gain_two = gains[0:1, :], gains[1:2, :]
@@ -595,6 +595,7 @@
     for back in (0,) + order[:2]:
         from_diag(0, back)
     lax.fori_loop(0, blocks, positions, 0)
+    place_slots(4, small_s, slot, slot_rows)
     from_diag(0, order[2])
     core_columns = (across, x_dev + across - dp, y_dev + across - dp, diag + across - dp)
 
@@ -710,7 +711,6 @@
     lax.fori_loop(0, blocks, after, 0)
     abroad(spread_far, 2)
     abroad(expert_relay, 1)
-    place_slots(4, small_s, slot, slot_rows)
     for copy in flush(21, FRONT_KEPT):
         copy.start()
 
@@ -724,29 +724,41 @@
     last_half = remote(
         last_sent.at[some], came.at[3, some], row_send.at[4], row_recv.at[3], (across, next_z)
     )
+    def kinds_out(k):
+        device = ((dp, next_z), (across, z), (across, next_z))[k - 1]
+        return remote(
+            sent_kinds.at[k], came_kinds.at[k], row_send.at[4 + k], row_recv.at[3 + k], device
+        )
+
+    own_kinds = pltpu.make_async_copy(sent_kinds.at[0], came_kinds.at[0], row_send.at[8])
+
     def fill(n, carry):
         k = (n + 1) % 4
         eid = (z + k) % 2 + 2 * ((core + k // 2) % 2)
-        fill_slots(eid, gate, act_two, dy_s, mask, slot_rows, sent.at[k % 3])
+        fill_slots(eid, gate, act_two, dy_s, mask, slot_rows, sent.at[k % 3], sent_kinds.at[k])
 
         @pl.when(n == 0)
         def _():
+            kinds_out(1).start()
             rows_out(1).start()
 
         @pl.when(n == 1)
         def _():
+            kinds_out(2).start()
             rows_out(2).start()
 
         @pl.when(n == 2)
         def _():
             last_local.start()
             last_local.wait()
+            kinds_out(3).start()
             last_half.start()
 
         return carry
 
     lax.fori_loop(0, 4, fill, 0)
     own_local.start()
+    own_kinds.start()
     abroad(expert_relay, 2)
     for c in range(len(chunks)):
         expert_finish(c)
@@ -756,6 +768,10 @@
     last_half.wait_recv()
     last_half.wait_send()
     own_local.wait()
+    own_kinds.wait()
+    for k in (1, 2, 3):
+        kinds_out(k).wait_recv()
+        kinds_out(k).wait_send()
 
     def attn_sent(n, carry):
         for p in range(2):
@@ -1153,14 +1169,24 @@
     slot_rows[...] = slot[...].T
 
 
-def fill_slots(eid, gate, act_two, dy_s, mask, slot_rows, target):
+def adapter_pattern(rows, cols, first):
+    lanes = iota((rows, cols), 1)
+    start = ADAPTER_RANK * iota((rows, cols), 0)
+    return hot_matrix((lanes == start) if first else ((lanes - start) // ADAPTER_RANK == 0) & (lanes >= start))
+
+
+def fill_slots(eid, gate, act_two, dy_s, mask, slot_rows, target, kinds_target=None):
     row = slot_rows[pl.ds(eid, 1), :].astype(jnp.int32)
     pick = hot_matrix(row == iota((target.shape[0], row.shape[1]), 0))
     value = lane_value(gate[...], eid)
     scaled = (dy_s[...].astype(F32) * value).astype(BF16)
     target[:, :MODEL_WIDTH] = dot(pick, act_two[...]).astype(BF16)
     target[:, MODEL_WIDTH : 2 * MODEL_WIDTH] = dot(pick, scaled).astype(BF16)
-    target[:, 2 * MODEL_WIDTH :] = dot(pick, mask[...]).astype(BF16)
+    if kinds_target is None:
+        target[:, 2 * MODEL_WIDTH :] = dot(pick, mask[...]).astype(BF16)
+    else:
+        owner = dot_nt(adapter_pattern(kinds_target.shape[0], LANES, True), mask[...]).astype(BF16)
+        kinds_target[:, : target.shape[0]] = dot_nt(owner, pick).astype(BF16)
 
 
 def dispatch_body(experts, eids, small_s, gate, act_two, dy_s, mask, slot, sent, slot_rows):
@@ -1231,7 +1257,7 @@
 
 
 def pair_ffn_body(
-    had, last_sent, wide, mid, thin,
+    had, last_sent, kinds, wide, mid, thin,
     returned, out_ga_gu, out_gb_gu, out_ga_dn, out_gb_dn,
     came, back, ga_gu, gb_gu, ga_dn, gb_dn, w_gu, w_dn, a_gu, b_gu, a_dn, b_dn, acc_out, acc_dx, acc_low, acc_dlow,
     load_sems, came_sems, back_sems, done_sems, last_sems,
@@ -1303,8 +1329,8 @@
             last_out.wait_recv()
 
         back[k, :, :MODEL_WIDTH], back[k, :, MODEL_WIDTH:] = ffn_math(
-            came[k, :, :MODEL_WIDTH], came[k, :, MODEL_WIDTH : 2 * MODEL_WIDTH],
-            came[k, :, 2 * MODEL_WIDTH :].astype(F32), w_gu, w_dn, a_gu, b_gu, a_dn, b_dn,
+            came[k, :, :MODEL_WIDTH], came[k, :, MODEL_WIDTH:],
+            dot_tn(kinds[k, :, : came.shape[1]], adapter_pattern(kinds.shape[1], LANES, False)), w_gu, w_dn, a_gu, b_gu, a_dn, b_dn,
             ga_gu, gb_gu, ga_dn, gb_dn, acc_out, acc_dx, acc_low, acc_dlow,
         )
 
@@ -1381,7 +1407,7 @@
     for n, factor in enumerate(factors):
         columns = jnp.where(spot == n, factor, columns)
     columns = columns.T
-    v_zero, v_one = const_value[0:1, :], const_value[1:2, :]
+    v_zero, v_one = const_value[0:1, :].astype(F32), const_value[1:2, :].astype(F32)
     out = res + columns[:, 0:1] * act + columns[:, 1:2] * v_zero + columns[:, 2:3] * v_one
     d_act = columns[:, 0:1] * dy
     met = jnp.where(lane == 0, jnp.sum(dy * act, axis=1, keepdims=True), 0.0)
@@ -1560,7 +1586,6 @@
     )
     gains = jnp.stack([attention_gain, feedfwd_gain])
     gain_one, gain_two = gains[0:1], gains[1:2]
-    const_value = constant_value.astype(F32)
     sent_width = 2 * width + LANES
     full = whole
     hbm = pl.BlockSpec(memory_space=pl.ANY)
@@ -1587,31 +1612,33 @@
             (gu_rows + up_rows, 2 * FEEDFWD_WIDTH), (dn_rows + up_rows, width),
             (gu_rows + dn_rows, LANES),
         ]
-        row_shape = (expert_count, cap, sent_width)
+        row_shape = (expert_count, cap, 2 * width)
+        kinds_shape = (expert_count, 16, -(-cap // LANES) * LANES)
         (
             hid_s, dy_s, small_s, act_one, low_qkv, mask, starts, cosine, sine, router,
             query, key, value, w_qkv, a_qkv, b_qkv, w_out, a_out, b_out,
             attn_low, lse, low_out, resid, act_two, gate, slot,
-            wide, mid, thin, came, last_sent,
+            wide, mid, thin, came, last_sent, came_kinds,
         ) = pl.pallas_call(
             functools.partial(pair_front_body, kinds, a_rows, b_rows),
             in_specs=[smem] * 2 + [vmem] * 14 + [hbm] * 6,
-            out_specs=[hbm] * (FRONT_KEPT + 5),
+            out_specs=[hbm] * (FRONT_KEPT + 6),
             out_shape=shapes
             + [sds((dp_size,) + shape, BF16) for shape in packed]
-            + [sds(row_shape, BF16), sds(row_shape[1:], BF16)],
+            + [sds(row_shape, BF16), sds(row_shape[1:], BF16), sds(kinds_shape, BF16)],
             scratch_shapes=[pltpu.VMEM(s.shape, s.dtype) for s in shapes]
             + [
                 pltpu.VMEM((devices, shard_rows, 3 * width + LANES), BF16),
                 pltpu.VMEM((devices, shard_rows, width + LANES), BF16),
                 *[pltpu.VMEM(shape, BF16) for shape in packed],
                 pltpu.VMEM((3,) + row_shape[1:], BF16),
+                pltpu.VMEM(kinds_shape, BF16),
                 pltpu.VMEM((LANES, tok), F32),
                 pltpu.SemaphoreType.DMA((2, 35)), pltpu.SemaphoreType.DMA((2, 35)),
                 pltpu.SemaphoreType.DMA((2, 6)),
                 pltpu.SemaphoreType.DMA((4, 8)), pltpu.SemaphoreType.DMA((4, 8)),
                 pltpu.SemaphoreType.DMA((FRONT_KEPT,)), pltpu.SemaphoreType.DMA((6,)),
-                pltpu.SemaphoreType.DMA((5,)), pltpu.SemaphoreType.DMA((4,)),
+                pltpu.SemaphoreType.DMA((9,)), pltpu.SemaphoreType.DMA((7,)),
             ],
             compiler_params=pltpu.CompilerParams(
                 vmem_limit_bytes=VMEM_BYTES, collective_id=4, has_side_effects=True
@@ -1733,12 +1760,12 @@
     if plan.paired:
         returned, ga_gu, gb_gu, ga_dn, gb_dn = pl.pallas_call(
             pair_ffn_body,
-            in_specs=[hbm] * 5,
+            in_specs=[hbm] * 2 + [vmem] + [hbm] * 3,
             out_specs=[hbm] + [vmem] * 4,
             out_shape=[sds((expert_count, cap, 2 * width), BF16)]
             + [sds(g.shape, BF16) for g in grad_shapes],
             scratch_shapes=[
-                pltpu.VMEM((expert_count, cap, sent_width), BF16),
+                pltpu.VMEM((expert_count, cap, 2 * width), BF16),
                 pltpu.VMEM((expert_count, cap, 2 * width), BF16),
                 *[pltpu.VMEM(g.shape, F32) for g in grad_shapes],
                 pltpu.VMEM((width, 2 * FEEDFWD_WIDTH), BF16), pltpu.VMEM((FEEDFWD_WIDTH, width), BF16),
@@ -1753,7 +1780,7 @@
                 vmem_limit_bytes=VMEM_BYTES, collective_id=1, has_side_effects=True
             ),
             name="pair_ffn",
-        )(came, last_sent, wide, mid, thin)
+        )(came, last_sent, came_kinds, wide, mid, thin)
     else:
         w_gu = wide[:, :gu_rows].reshape(width, 2 * FEEDFWD_WIDTH)
         b_gu = wide[:, gu_rows:].reshape(LANES, 2 * FEEDFWD_WIDTH)
@@ -1789,7 +1816,7 @@
          sds((tok, LANES), F32), sds((width, LANES), F32), sds((LANES, width), F32)],
         name="combine",
     )(eids, resid, act_two, dy_s, gate, slot, small_s, low_out, attn_low, mask, returned,
-      w_out, a_out, b_out, router, const_value, gain_two)
+      w_out, a_out, b_out, router, constant_value, gain_two)
 
     if plan.paired:
         flow = dict(vmem_limit_bytes=VMEM_BYTES, has_side_effects=True)

time: 347 us -> 345 us (level)
  no operation moved by 1% of the time
where the time goes in v3:
time: 345 us; the launch traced here: 339 us
  Pallas kernels  335 us (97%)
    pallas_call x1, Pallas kernels, shards(): pl.pallas_call(functools.partial(pair_front_body, kinds, a_rows, b_rows),...  139 us
    pallas_call x1, Pallas kernels, shards(): pl.pallas_call(pair_ffn_body, in_specs=[hbm] * 2 + [vmem] + [hbm] * 3, ou...  80.4 us
    pallas_call x1, Pallas kernels, shards(): pl.pallas_call(pair_attention_bwd_body, grid=(pairs,), in_specs=[col_spec...  47.9 us
    pallas_call x1, Pallas kernels, shards(): pl.pallas_call(pair_tail_body, in_specs=[vmem] * 8 + [hbm] * 9, out_specs...  34.3 us
    pallas_call x1, Pallas kernels, shards(): call(functools.partial(combine_body, expert_count, kinds), (tok // ROW_BL...  26.5 us
    pallas_call x1, Pallas kernels, shards(): call(settle_body, (blocks,), [row_spec(LANES), row_spec(width), row_spec(...  7.33 us

profile of v3, /device:TPU:1, one launch (start us, length us, event | category | flops | bytes accessed | tf_op | source)
XLA Modules:
  0.0 338.7 jit_solution(9662823138931788066)
XLA Ops:
  0.6 0.7 stack.10.gain
  1.3 0.0 copy-start.1
  1.3 0.7 stack.9.gain
  2.0 0.0 copy-start
  2.0 0.6 pad_maximum_fusion.gains
  2.6 138.8 %pair_front.1 = (bf16[1280,768]{1,0:T(8,128)(2,1)}, bf16[1280,768]{1,0:T(8,128)(2,1)}, f32[1280,128]{1,0:T(8,128)}, bf16[1280,768]{1,0:T(8,128)(2,1)}, bf16[1280...) custom-call(s32[1,5]{1,0:T(1,128)} %lengths.1, ...), custom_call_target="tpu_custom_call" | custom-call | tf_op jit(solution)/shard_map/pair_front/pallas_call | solution.py:1622
  141.4 0.0 copy-done.1
  141.4 0.0 copy-done
  141.4 80.4 %pair_ffn.1 = (bf16[4,416,1536]{2,1,0:T(8,128)(2,1)}, bf16[768,128]{1,0:T(8,128)(2,1)}, bf16[128,4096]{1,0:T(8,128)(2,1)}, bf16[2048,128]{1,0:T(8,128)(2,1)}, bf16[128,768]{1,0:T(8,128)(2,1)}) custom-call(bf16[4,416,1536]{2,1,0:T(8,128)(2,1)} %get-tuple-element.95.had, bf16[416,1536]{1,0:T(8,128)(2,1)} %get-tuple-element.96.last_sent, ...), custom_call_target="tpu_custom_call" | custom-call | tf_op jit(solution)/shard_map/pair_ffn/pallas_call | solution.py:1761
  221.8 0.5 iota_xor_fusion.eids
  222.3 26.5 %combine.1 = (bf16[1280,768]{1,0:T(8,128)(2,1)}, f32[1280,768]{1,0:T(8,128)}, bf16[1280,768]{1,0:T(8,128)(2,1)}, f32[1280,128]{1,0:T(8,128)}, f32[768,128]{1,0:T(8,128)}, /*index=5*/f32[128,768]{1,0:T(8,128)}) custom-call(s32[4]{0:T(128)} %iota_xor_fusion.eids, f32[1280,768]{1,0:T(8,128)} %get-tuple-element.87.resid, ...), custom_call_target="tpu_custom_call" | custom-call | tf_op jit(solution)/shard_map/combine/pallas_call | solution.py:1806
  248.9 47.9 %pair_attention_bwd.1 = (bf16[1280,768]{1,0:T(8,128)(2,1)}, bf16[1280,768]{1,0:T(8,128)(2,1)}, bf16[1280,768]{1,0:T(8,128)(2,1)}, f32[96,128]{1,0:T(8,128)}, f32...) custom-call(bf16[1280,768]{1,0:T(8,128)(2,1)} %get-tuple-element.84.quer, ...), custom_call_target="tpu_custom_call" | custom-call | tf_op jit(solution)/shard_map/pair_attention_bwd/pallas_call | solution.py:1830
  296.8 34.3 %pair_tail.1 = (bf16[1280,768]{1,0:T(8,128)(2,1)}, f32[1280,768]{1,0:T(8,128)}, f32[1280,128]{1,0:T(8,128)}, f32[24,128]{1,0:T(8,128)}, f32[4,2304]{1,0:T(4,128)}, /*index=5*/f32[24,128]{1,0:T(8,128)}, f32[4,768]{1,0:T(4,128)}) custom-call(s32[1,1280]{1,0:T(1,128)} %place_row.3, bf16[1280,128]{1,0:T(8,128)(2,1)} %get-tuple-element.81.mask, ...), custom_call_target="tpu_custom_call" | custom-call | tf_op jit(solution)/shard_map/pair_tail/pallas_call | solution.py:1861
  331.1 7.3 %settle.1 = (f32[8,1280]{1,0:T(8,128)}, bf16[1280,768]{1,0:T(8,128)(2,1)}, f32[1280,768]{1,0:T(8,128)}, f32[24,128]{1,0:T(8,128)}, f32[4,2304]{1,0:T(4,128)}, /*...) custom-call(f32[1280,128]{1,0:T(8,128)} %get-tuple-element.129.refs_, ...), custom_call_target="tpu_custom_call" | custom-call | tf_op jit(solution)/shard_map/settle/pallas_call | solution.py:1892
Async XLA Ops:
  1.3 140.1 %copy-start.1 = (bf16[1,768]{1,0:T(2,128)(2,1)}, bf16[1,768]{1,0:T(2,128)(2,1)S(1)}, u32[]{:S(2)}) copy-start(bf16[1,768]{1,0:T(2,128)(2,1)S(1)} %stack.10.gain) | copy-start | bytes 4612
  2.0 139.4 %copy-start = (bf16[1,768]{1,0:T(2,128)(2,1)}, bf16[1,768]{1,0:T(2,128)(2,1)S(1)}, u32[]{:S(2)}) copy-start(bf16[1,768]{1,0:T(2,128)(2,1)S(1)} %stack.9.gain) | copy-start | bytes 4612
